TPU v7x, 256 devices: a whole 4x4x8 slice. The times are simulated.
256 devices in a mesh: group: 2 (over y_lo), seq: 16 (over z, y_hi), fsdp: 8 (over x, core).
Axes of the slice: x: 4, y: 4 (y_hi: 2, y_lo: 2; y = y_hi * 2 + y_lo), z: 8, core: 2. Of those that a mesh axis runs over, the one named last changes fastest.
Arguments:
- block_input: bfloat16 [2, 4096, 2560], P('group', 'seq', 'fsdp'), may hold values from -60 to 60
- head_outputs: bfloat16 [2, 4096, 3072], P('group', 'seq'), may hold values from -6 to 6
- out_master: float32 [2, 3072, 2560], P('group', 'seq', 'fsdp'), may hold values from -0.109375 to 0.109375
- first_moment: float32 [2, 3072, 2560], P('group', 'seq', 'fsdp'), may hold values from -3 to 3
- second_moment: float32 [2, 3072, 2560], P('group', 'seq', 'fsdp'), may hold values from 0.5 to 2
- score_qkv: bfloat16 [2, 3, 3072, 2560], P('group', None, 'fsdp', 'seq'), may hold values from -0.125 to 0.125
- teacher_out: bfloat16 [3072, 2560], P('seq', 'fsdp'), may hold values from -0.109375 to 0.109375
- noise: bfloat16 [4096, 2560], P('seq', 'fsdp'), may hold values from -6 to 6
- timestep: int32 [1], replicated, may hold values from 300 to 700
- fake_target: bfloat16 [4096, 2560], P('seq', 'fsdp'), may hold values from -6 to 6
Outputs:
- new_master: float32 [2, 3072, 2560], P('group', 'seq', 'fsdp')
- new_first: float32 [2, 3072, 2560], P('group', 'seq', 'fsdp')
- new_second: float32 [2, 3072, 2560], P('group', 'seq', 'fsdp')
All inputs are finite; a program needn't handle non-finite values. Where the computation divides by a largest or mean magnitude, that divisor is 1e-20 or more.
Results may differ from a plain program's by a relative error of at most 0.0075.
Values may be sent and summed in bfloat16 or wider, within the bound.
A program may use at most 64 MiB of HBM per device.

v0:
```python
import math

import jax
import jax.numpy as jnp
from jax import lax
from jax.sharding import PartitionSpec as P

D = 2560
HEAD_DIM = 128


norm_eps = 1e-06
first_fix = 1.0 - 0.9**20
second_fix = 1.0 - 0.95**20
learn_rate = 0.003


def passed_along(value, axis, by):
    length = lax.axis_size(axis)
    pairs = [(i, i + by) for i in range(length) if 0 <= i + by < length]
    return lax.ppermute(value, axis, pairs)


def head_norm(projected):
    shaped = projected.reshape(projected.shape[0], -1, HEAD_DIM)
    factor = lax.rsqrt(jnp.mean(shaped * shaped, axis=2, keepdims=True) + norm_eps)
    return (shaped * factor).reshape(projected.shape).astype(jnp.bfloat16)


def attend_block(query_shaped, key_shaped, value_shaped):
    scores = jnp.einsum(
        "qhd,khd->hqk", query_shaped, key_shaped, preferred_element_type=jnp.float32
    ) * (1.0 / math.sqrt(HEAD_DIM))
    weights = jnp.exp(scores)
    numerator = jnp.einsum(
        "hqk,khd->qhd",
        weights.astype(jnp.bfloat16),
        value_shaped,
        preferred_element_type=jnp.float32,
    )
    return (numerator, jnp.sum(weights, axis=2).T)


def add_heads(left_rows, shard_piece):
    return jnp.dot(left_rows, shard_piece, preferred_element_type=jnp.float32)


def body(
    block_input,
    head_outputs,
    out_master,
    first_moment,
    second_moment,
    score_qkv,
    teacher_out,
    noise,
    timestep,
    fake_target,
):
    first_group = lax.axis_index("group") == 0
    tokens_here = block_input.shape[1]
    local_inner = score_qkv.shape[2]
    local_heads = local_inner // HEAD_DIM
    rows_total = tokens_here * lax.axis_size("seq")
    work_weight = out_master[0].astype(jnp.bfloat16)
    out_pick = jnp.where(first_group, teacher_out, work_weight)
    own_heads = head_outputs[0]
    branch_first = add_heads(own_heads, lax.all_gather(work_weight, "seq", axis=0, tiled=True))
    predicted = block_input[0].astype(jnp.float32) + branch_first
    generated = predicted.astype(jnp.bfloat16)
    arrived = passed_along(generated, "group", 1)
    source = jnp.where(first_group, generated, arrived)
    noise_level = timestep[0].astype(jnp.float32) / 1000.0
    noisy_rows = (
        (1.0 - noise_level) * source.astype(jnp.float32) + noise_level * noise.astype(jnp.float32)
    ).astype(jnp.bfloat16)
    gathered = lax.all_gather(noisy_rows, "fsdp", axis=1, tiled=True)
    widened = gathered.astype(jnp.float32)
    normed = (
        widened * lax.rsqrt(jnp.mean(widened * widened, axis=1, keepdims=True) + norm_eps)
    ).astype(jnp.bfloat16)
    projected = jnp.einsum(
        "td,cid->cti",
        normed,
        lax.all_gather(score_qkv[0], "seq", axis=2, tiled=True),
        preferred_element_type=jnp.float32,
    )
    query_hat = head_norm(projected[0])
    key_hat = head_norm(projected[1])
    value_rows = projected[2].astype(jnp.bfloat16)
    query_shaped = query_hat.reshape(tokens_here, local_heads, HEAD_DIM)
    start_state = (
        jnp.zeros((tokens_here, local_heads, HEAD_DIM), jnp.float32),
        jnp.zeros((tokens_here, local_heads), jnp.float32),
    )
    key_piece = lax.all_gather(key_hat, "seq", axis=0, tiled=True)
    value_piece = lax.all_gather(value_rows, "seq", axis=0, tiled=True)
    key_count = key_piece.shape[0]
    block_size = math.gcd(key_count, 512)
    key_blocks = key_piece.reshape(key_count // block_size, block_size, local_heads, HEAD_DIM)
    value_blocks = value_piece.reshape(key_count // block_size, block_size, local_heads, HEAD_DIM)

    def advance(running, blocks):
        numerator, weight_sum = attend_block(query_shaped, blocks[0], blocks[1])
        return ((running[0] + numerator, running[1] + weight_sum), None)

    result, unused_out = lax.scan(advance, start_state, (key_blocks, value_blocks))
    numerator, weight_sum = result
    attended = (
        (numerator / weight_sum[:, :, None]).reshape(tokens_here, local_inner).astype(jnp.bfloat16)
    )
    all_heads = lax.all_gather(attended, "fsdp", axis=1, tiled=True)
    branch_second = add_heads(all_heads, lax.all_gather(out_pick, "seq", axis=0, tiled=True))
    teacher_guess = noisy_rows.astype(jnp.float32) + branch_second
    gap_total = lax.psum(
        jnp.sum(jnp.abs(source.astype(jnp.float32) - teacher_guess)), ("seq", "fsdp")
    )
    gap_mean = gap_total / (rows_total * D)
    fake_branch = passed_along(branch_second, "group", -1)
    match_grad = (fake_branch - branch_second) / (gap_mean + norm_eps)
    regress_grad = (predicted - fake_target.astype(jnp.float32)) / math.sqrt(rows_total)
    grad_rows = jnp.where(first_group, match_grad, regress_grad).astype(jnp.bfloat16)
    weight_grad = lax.psum_scatter(
        lax.dot_general(
            own_heads, grad_rows, (((0,), (0,)), ((), ())), preferred_element_type=jnp.float32
        ),
        "seq",
        scatter_dimension=0,
        tiled=True,
    )
    new_first = 0.9 * first_moment[0] + 0.1 * weight_grad
    new_second = 0.95 * second_moment[0] + 0.05 * weight_grad * weight_grad
    new_master = out_master[0] - learn_rate * (new_first / first_fix) / (
        jnp.sqrt(new_second / second_fix) + 1e-08
    )
    return (new_master[None], new_first[None], new_second[None])


def solution(mesh):
    placed = (
        P("group", "seq", "fsdp"),
        P("group", "seq", None),
        P("group", "seq", "fsdp"),
        P("group", "seq", "fsdp"),
        P("group", "seq", "fsdp"),
        P("group", None, "fsdp", "seq"),
        P("seq", "fsdp"),
        P("seq", "fsdp"),
        P(),
        P("seq", "fsdp"),
    )
    return jax.shard_map(
        body,
        mesh=mesh,
        in_specs=placed,
        out_specs=(P("group", "seq", "fsdp"), P("group", "seq", "fsdp"), P("group", "seq", "fsdp")),
        check_vma=False,
    )
```

profile of v0, /device:TPU:1, one launch (start us, length us, event | category | flops | bytes accessed | tf_op | source)
XLA Modules:
  0.0 1116.9 jit_solution(9206541233786530961)
XLA Ops:
  7.2 1.9 broadcast_select_fusion.1
  9.2 89.8 %all-gather.10.cloned.1.call-done = bf16[3072,320]{1,0:T(8,128)(2,1)} async-done(((bf16[192,320]{1,0:T(8,128)(2,1)}), bf16[3072,320]{1,0:T(8,128)(2,1)}) %all-gather.10.cloned.1.call-update) | async-done | bytes 1966096 | tf_op jit(solution)/shard_map/all_gather | solution.py:68
  99.0 2.7 fusion.38
  101.7 2.2 collective-permute-start
  104.5 1.6 collective-permute-done
  106.1 0.7 fusion.25
  107.7 29.5 %all-gather.12.cloned.1.call-done = bf16[256,2560]{0,1:T(8,128)(2,1)} async-done(((bf16[256,320]{0,1:T(8,128)(2,1)}), bf16[256,2560]{0,1:T(8,128)(2,1)}) %all-gather.12.cloned.1.call-update) | async-done | bytes 1310736 | tf_op jit(solution)/shard_map/all_gather | solution.py:77
  137.2 1.7 fusion.9
  138.9 110.7 %all-gather.20.cloned.1.call-done = bf16[1,3,384,2560]{2,3,1,0:T(8,128)(2,1)} async-done(((bf16[1,3,384,160]{2,3,1,0:T(8,128)(2,1)}), bf16[1,3,384,2560]{2,3,1,0:T(8,128)(2,1)}) %all-gather.20.cloned.1.call-update) | async-done | bytes 5898256 | tf_op jit(solution)/shard_map/all_gather | solution.py:85
  249.6 5.0 fusion.14
  254.6 0.9 fusion.37
  255.5 1.2 copy.49
  256.8 0.9 copy.50
  257.7 1.7 fusion.23
  260.9 1.2 copy.52
  262.1 0.8 copy.55
  263.0 85.3 %all-gather.14.cloned.1.call-done = bf16[4096,384]{1,0:T(8,128)(2,1)} async-done(((bf16[256,384]{1,0:T(8,128)(2,1)}), bf16[4096,384]{1,0:T(8,128)(2,1)}) %all-gather.14.cloned.1.call-update) | async-done | bytes 3145744 | tf_op jit(solution)/shard_map/all_gather | solution.py:96
  348.3 9.0 reshape.66
  357.3 4.7 copy.54
  362.0 79.2 %all-gather.22.cloned.1.call-done = bf16[1,4096,384]{2,1,0:T(8,128)(2,1)} async-done(((bf16[1,256,384]{2,1,0:T(8,128)(2,1)}), bf16[1,4096,384]{2,1,0:T(8,128)(2,1)}) %all-gather.22.cloned.1.call-update) | async-done | bytes 3145744 | tf_op jit(solution)/shard_map/all_gather | solution.py:97
  441.2 9.0 reshape.65
  450.2 7.2 copy.53
  457.4 22.6 %while.13 = (s32[]{:T(128)}, f32[256,3,128]{0,2,1:T(8,128)S(1)}, f32[256,3]{0,1:T(4,128)S(1)}, bf16[8,512,3,128]{1,3,2,0:T(8,128)(2,1)}, bf16[8,512,3,128]{3,1,2...) while((s32[]{:T(128)}, f32[256,3,128]{0,2,1:T(8,128)S(1)}, ...), condition=%wide.region_5.6_spmd.clone, body=%wide.region_3.5_spmd.clone.sunk | while | flops 202703616 | bytes 3355744 | solution.py:107
  457.4 1.5 bitcast_reduce_fusion.2
  458.9 1.3 fusion.51
  460.2 1.5 bitcast_reduce_fusion.2
  461.7 1.3 fusion.51
  463.1 1.5 bitcast_reduce_fusion.2
  464.6 1.3 fusion.51
  465.9 1.5 bitcast_reduce_fusion.2
  467.4 1.3 fusion.51
  468.7 1.5 bitcast_reduce_fusion.2
  470.2 1.3 fusion.51
  471.5 1.5 bitcast_reduce_fusion.2
  473.0 1.3 fusion.51
  474.4 1.5 bitcast_reduce_fusion.2
  475.8 1.3 fusion.51
  477.2 1.5 bitcast_reduce_fusion.2
  478.7 1.3 fusion.51
  480.8 47.1 %all-gather.18.cloned.1.call-done = bf16[3072,320]{1,0:T(8,128)(2,1)} async-done(((bf16[192,320]{1,0:T(8,128)(2,1)}), bf16[3072,320]{1,0:T(8,128)(2,1)}) %all-gather.18.cloned.1.call-update) | async-done | bytes 1966096 | tf_op jit(solution)/shard_map/all_gather | solution.py:113
  527.9 30.1 %all-gather.16.cloned.1.call-done = bf16[256,3072]{0,1:T(8,128)(2,1)} async-done(((bf16[256,384]{0,1:T(8,128)(2,1)}), bf16[256,3072]{0,1:T(8,128)(2,1)}) %all-gather.16.cloned.1.call-update) | async-done | bytes 1572880 | tf_op jit(solution)/shard_map/all_gather | solution.py:112
  558.0 3.8 fusion.27
  561.7 1.3 collective-permute-start.1
  563.0 324.0 %psum.7 = f32[]{:T(128)} all-reduce(f32[]{:T(128)} %get-tuple-element.106), channel_id=1, replica_groups=mesh['group'=2,'seq'=16,'fsdp'=8] {'seq','fsdp'}, use_global_device_ids=true, to_apply=%region_7.8 | all-reduce | flops 1 | bytes 8 | tf_op jit(solution)/shard_map/psum | solution.py:115
  887.6 2.6 convolution_bitcast_fusion.1
  890.3 5.7 copy.66
  896.0 212.0 %reduce-scatter.4.cloned.1.call-done = f32[192,320]{1,0:T(8,128)} async-done(((f32[3072,320]{1,0:T(8,128)}), f32[192,320]{1,0:T(8,128)}) %reduce-scatter.4.cloned.1.call-update) | async-done | bytes 245776 | tf_op jit(solution)/shard_map/reduce_scatter | solution.py:123
  1108.0 2.1 fusion.34
  (56 shorter events, 3.4 us)
Async XLA Ops:
  7.2 91.8 %copy-start = (bf16[1,256,3072]{2,1,0:T(8,128)(2,1)S(1)}, bf16[1,256,3072]{2,1,0:T(8,128)(2,1)}, u32[]{:S(2)}) copy-start(bf16[1,256,3072]{2,1,0:T(8,128)(2,1)} %param.13) | copy-start | bytes 4718596
  7.2 91.8 %all-gather.10.cloned.1.call-start = ((), (), s32[]{:S(2)}) async-start(), calls=%async_computation.1 | async-start | bytes 2506752 | tf_op jit(solution)/shard_map/all_gather | solution.py:68
  9.1 97.0 %copy-start.8 = (bf16[256,320]{0,1:T(8,128)(2,1)S(1)}, bf16[256,320]{0,1:T(8,128)(2,1)}, u32[]{:S(2)}) copy-start(bf16[256,320]{0,1:T(8,128)(2,1)} %param.19) | copy-start | bytes 491524
  9.1 128.1 %all-gather.12.cloned.1.call-start = ((), (), s32[]{:S(2)}) async-start(), calls=%async_computation.2 | async-start | bytes 1474560 | tf_op jit(solution)/shard_map/all_gather | solution.py:77
  101.6 37.3 %copy-start.2 = (bf16[256,320]{0,1:T(8,128)(2,1)}, bf16[256,320]{0,1:T(8,128)(2,1)S(1)}, u32[]{:S(2)}) copy-start(bf16[256,320]{0,1:T(8,128)(2,1)S(1)} %get-tuple-element.104) | copy-start | bytes 491524
  101.7 4.5 collective-permute-start
  106.1 32.8 %copy-start.9 = (bf16[256,320]{0,1:T(8,128)(2,1)}, bf16[256,320]{0,1:T(8,128)(2,1)S(1)}, u32[]{:S(2)}) copy-start(bf16[256,320]{0,1:T(8,128)(2,1)S(1)} %collective-permute-done) | copy-start | bytes 491524
  106.9 142.7 %all-gather.20.cloned.1.call-start = ((), (), s32[]{:S(2)}) async-start(), calls=%async_computation.6 | async-start | bytes 6266880 | tf_op jit(solution)/shard_map/all_gather | solution.py:85
  107.6 240.6 %all-gather.14.cloned.1.call-start = ((), (), s32[]{:S(2)}) async-start(), calls=%async_computation.3 | async-start | bytes 3342336 | tf_op jit(solution)/shard_map/all_gather | solution.py:96
  259.5 181.7 %all-gather.22.cloned.1.call-start = ((), (), s32[]{:S(2)}) async-start(), calls=%async_computation.7 | async-start | bytes 3342336 | tf_op jit(solution)/shard_map/all_gather | solution.py:97
  260.2 267.6 %all-gather.18.cloned.1.call-start = ((), (), s32[]{:S(2)}) async-start(), calls=%async_computation.5 | async-start | bytes 2506752 | tf_op jit(solution)/shard_map/all_gather | solution.py:113
  260.8 297.1 %all-gather.16.cloned.1.call-start = ((), (), s32[]{:S(2)}) async-start(), calls=%async_computation.4 | async-start | bytes 1769472 | tf_op jit(solution)/shard_map/all_gather | solution.py:112
  457.4 100.6 %copy-start.3 = (bf16[256,320]{0,1:T(8,128)(2,1)S(1)}, bf16[256,320]{0,1:T(8,128)(2,1)}, u32[]{:S(2)}) copy-start(bf16[256,320]{0,1:T(8,128)(2,1)} %copy-done.2) | copy-start | bytes 491524
  457.4 100.6 %copy-start.4 = (bf16[256,320]{0,1:T(8,128)(2,1)S(1)}, bf16[256,320]{0,1:T(8,128)(2,1)}, u32[]{:S(2)}) copy-start(bf16[256,320]{0,1:T(8,128)(2,1)} %fusion.25) | copy-start | bytes 491524
  480.7 406.9 %copy-start.5 = (bf16[256,320]{0,1:T(8,128)(2,1)S(1)}, bf16[256,320]{0,1:T(8,128)(2,1)}, u32[]{:S(2)}) copy-start(bf16[256,320]{0,1:T(8,128)(2,1)} %param.21) | copy-start | bytes 491524
  480.7 627.2 %reduce-scatter.4.cloned.1.call-start = ((), (), s32[]{:S(2)}) async-start(), calls=%async_computation.8 | async-start | bytes 5013504 | tf_op jit(solution)/shard_map/reduce_scatter | solution.py:123
  561.7 325.9 %collective-permute-start.1 = (f32[256,320]{0,1:T(8,128)S(1)}, f32[256,320]{0,1:T(8,128)S(1)}, u32[]{:S(2)}, u32[]{:S(2)}) collective-permute-start(f32[256,320]{0,1:T(8,128)S(1)} %get-tuple-element.107), channel_id=1, source_target_pairs={{128,0},{129,1},{130,2},{131,3},{132,4},{133,5},{134,6},{135,7},{1... | collective-permute-start | bytes 983048 | tf_op jit(solution)/shard_map/ppermute | solution.py:21
  896.0 212.0 %copy-start.1 = (f32[1,192,320]{2,1,0:T(8,128)S(1)}, f32[1,192,320]{2,1,0:T(8,128)}, u32[]{:S(2)}) copy-start(f32[1,192,320]{2,1,0:T(8,128)} %param.14) | copy-start | bytes 737284
  896.0 212.0 %copy-start.6 = (f32[1,192,320]{2,1,0:T(8,128)S(1)}, f32[1,192,320]{2,1,0:T(8,128)}, u32[]{:S(2)}) copy-start(f32[1,192,320]{2,1,0:T(8,128)} %param.16) | copy-start | bytes 737284
  896.0 212.0 %copy-start.7 = (f32[1,192,320]{2,1,0:T(8,128)S(1)}, f32[1,192,320]{2,1,0:T(8,128)}, u32[]{:S(2)}) copy-start(f32[1,192,320]{2,1,0:T(8,128)} %param.15) | copy-start | bytes 737284
Sparse Core Ops, SparseCore 0:
  11.2 87.7 all-gather.9
  107.0 30.1 all-gather.11
  139.8 109.7 all-gather.19
  259.6 88.6 all-gather.13
  351.3 89.8 all-gather.21
  443.6 84.1 all-gather.17
  530.3 27.6 all-gather.15
  896.1 211.7 reduce-scatter.3
where the time goes:
time: 1120 us
  waiting for transfers between devices  687 us (61%)
  blocking collectives  324 us (29%)
  local copies, waits for them, and re-layouts  40.4 us (4%)
  matrix products  36.3 us (3%)
  between operations  15.6 us (1%)
    psum x1, blocking collectives, body(): lax.psum(jnp.sum(jnp.abs(source.astype(jnp.float32) - teacher_guess)), ('...  324 us
    reduce_scatter x1, waiting for transfers between devices, body(): lax.psum_scatter(lax.dot_general(own_heads, grad_rows, (((0,), (0,)), (()...  212 us
    all_gather x1, waiting for transfers between devices, body(): lax.all_gather(score_qkv[0], 'seq', axis=2, tiled=True)  111 us
    all_gather x1, waiting for transfers between devices, body(): lax.all_gather(work_weight, 'seq', axis=0, tiled=True)  89.8 us
    all_gather x1, waiting for transfers between devices, body(): key_piece = lax.all_gather(key_hat, 'seq', axis=0, tiled=True)  85.3 us
    all_gather x1, waiting for transfers between devices, body(): value_piece = lax.all_gather(value_rows, 'seq', axis=0, tiled=True)  79.2 us
    all_gather x1, waiting for transfers between devices, body(): lax.all_gather(out_pick, 'seq', axis=0, tiled=True)  47.1 us
    all_gather x1, waiting for transfers between devices, body(): all_heads = lax.all_gather(attended, 'fsdp', axis=1, tiled=True)  30.1 us
  transfers between devices with their start and end apart: 10, of which 9 were waited for; matrix products, arithmetic and copies ran while one was open for 5% of the time, Pallas kernels for 0%

commit v1 on v0

v1 whole, which is shorter than its diff:
```python
import functools
import math

import jax
import jax.numpy as jnp
from jax import lax
from jax.experimental import pallas as pl
from jax.experimental.pallas import tpu as pltpu
from jax.sharding import PartitionSpec as P

D = 2560
HEAD_DIM = 128
MESH = pl.DeviceIdType.MESH

norm_eps = 1e-06
first_fix = 1.0 - 0.9**20
second_fix = 1.0 - 0.95**20
learn_rate = 0.003


class Sends:
    def __init__(self):
        self.open = []

    def start(self, ends, send_sem, recv_sem, device, when=None):
        def make():
            src, dst = ends()
            return pltpu.make_async_remote_copy(
                src_ref=src,
                dst_ref=dst,
                send_sem=send_sem(),
                recv_sem=recv_sem(),
                device_id=device(),
                device_id_type=MESH,
            )

        make().start()
        self.open.append((make, when))

    def same(self, ref, send_sem, recv_sem, device, when=None):
        def ends():
            here = ref()
            return here, here

        self.start(ends, send_sem, recv_sem, device, when)

    def finish(self):
        for make, when in self.open:
            if when is None:
                make().wait_send()
            else:
                pl.when(when)(lambda make=make: make().wait_send())
        self.open = []


def wait_recv(dst, recv_sem):
    pltpu.make_async_copy(dst, dst, recv_sem).wait()


class Ring:
    def __init__(self, sends, place, buf, rows, sems, when=None):
        self.sends, self.place, self.buf, self.rows, self.when = sends, place, buf, rows, when
        self.ring_send, self.ring_recv, self.pair_send, self.pair_recv = sems
        self.steps = place.zs // 2

    def piece(self, zz, cc, half):
        each = self.rows // 2
        start = (2 * zz + cc) * self.rows + half * each
        return self.buf.at[pl.ds(pl.multiple_of(start, 16), each)]

    def parts(self, k):
        if k < self.steps:
            return [(0, 0), (1, 0), (0, 1), (1, 1)]
        return [(0, 0), (1, 1)]

    def zz(self, k, way):
        p = self.place
        return lax.rem(p.z + p.zs - k, p.zs) if way == 0 else lax.rem(p.z + k, p.zs)

    def send(self, k, way, half):
        p = self.place
        self.sends.same(
            lambda: self.piece(self.zz(k - 1, way), p.c, half),
            lambda: self.ring_send.at[k - 1, way, half],
            lambda: self.ring_recv.at[k - 1, way, half],
            lambda: p.dev(z=p.zp if way == 0 else p.zm),
            self.when,
        )

    def pair(self, k, way, half):
        p = self.place
        self.sends.same(
            lambda: self.piece(self.zz(k, way), p.c, half),
            lambda: self.pair_send.at[k, way, half],
            lambda: self.pair_recv.at[k, way, half],
            lambda: p.dev(c=1 - p.c),
            self.when,
        )

    def begin(self):
        for way, half in self.parts(1):
            self.send(1, way, half)
        for half in (0, 1):
            self.pair(0, 0, half)

    def advance(self, k):
        for way, half in self.parts(k):
            wait_recv(
                self.piece(self.zz(k, way), self.place.c, half),
                self.ring_recv.at[k - 1, way, half],
            )
            if k < self.steps and (way, half) in self.parts(k + 1):
                self.send(k + 1, way, half)
            self.pair(k, way, half)

    def pair_arrived(self, k):
        for way, half in self.parts(k) if k else [(0, 0), (0, 1)]:
            wait_recv(
                self.piece(self.zz(k, way), 1 - self.place.c, half),
                self.pair_recv.at[k, way, half],
            )


class Place:
    def __init__(self, zs, xs):
        self.zs, self.xs = zs, xs
        seq, fsdp = lax.axis_index("seq"), lax.axis_index("fsdp")
        self.g = lax.axis_index("group")
        self.z, self.a = seq // 2, lax.rem(seq, 2)
        self.x, self.c = fsdp // 2, lax.rem(fsdp, 2)
        self.zp = lax.rem(self.z + 1, zs)
        self.zm = lax.rem(self.z + zs - 1, zs)
        self.block = 2 * self.x + self.a
        self.kept = self.a == self.c
        self.moved = self.a != self.c

    def dev(self, g=None, z=None, a=None, x=None, c=None):
        g = self.g if g is None else g
        z = self.z if z is None else z
        a = self.a if a is None else a
        x = self.x if x is None else x
        c = self.c if c is None else c
        return {"group": g, "seq": 2 * z + a, "fsdp": 2 * x + c}

    def fan(self):
        return [(2 * dx + da, dx, da) for dx in range(self.xs) for da in range(2) if dx or da]

    def beside(self, dx, da):
        return self.dev(x=lax.rem(self.x + dx, self.xs), a=lax.rem(self.a + da, 2))


def kernel(
    zs,
    xs,
    ts_ref,
    bi_ref,
    ho_ref,
    ww_ref,
    qw_ref,
    to_ref,
    noise_ref,
    target_ref,
    out_ref,
    w_buf,
    q_buf,
    hob,
    bi_t,
    noise_t,
    target_t,
    gen,
    gen_in,
    noisy,
    norm,
    kv,
    q_hat,
    acc,
    lsum,
    att,
    pred,
    b_own,
    b_in,
    grad,
    tmp,
    rs_send,
    rs_recv,
    gap_f,
    gap_z,
    gap_c,
    wg_out,
    wg_in,
    t_send,
    t_recv,
    ho_send,
    ho_recv,
    ring_send,
    ring_recv,
    pair_send,
    pair_recv,
    fan_send,
    fan_recv,
    rs_ssem,
    rs_rsem,
    gz_send,
    gz_recv,
    one_send,
    one_recv,
    local_sem,
):
    p = Place(zs, xs)
    sends = Sends()
    tokens, inner = ho_ref.shape
    cols = bi_ref.shape[1]
    rows = ww_ref.shape[0]
    depth = qw_ref.shape[0]
    local_inner = q_hat.shape[1]
    heads = local_inner // HEAD_DIM
    steps = zs // 2
    fans = 2 * xs
    first = p.g == 0
    second = p.g == 1
    f32 = jnp.float32

    barrier = pltpu.get_barrier_semaphore()
    peers = [p.dev(z=lax.rem(p.z + dz, zs)) for dz in range(1, zs)]
    peers += [p.beside(dx, da) for _, dx, da in p.fan()]
    peers += [p.dev(c=1 - p.c), p.dev(g=1 - p.g), p.dev(a=1 - p.a, c=1 - p.c)]
    for peer in peers:
        pl.semaphore_signal(barrier, inc=1, device_id=peer, device_id_type=MESH)

    own_ho = pltpu.make_async_copy(ho_ref, hob.at[p.a], local_sem.at[0])
    own_ho.start()
    pl.semaphore_wait(barrier, len(peers))

    def rows_of(buf, each, at):
        return buf.at[pl.ds(pl.multiple_of(at * each, 16), each)]

    away, home = 2 * p.z + p.a, 2 * p.z + p.c
    swaps = [
        (ww_ref, lambda i: rows_of(w_buf.at[0], rows, i)),
        (bi_ref, lambda i: bi_t),
        (qw_ref, lambda i: rows_of(q_buf, depth, i)),
        (noise_ref, lambda i: noise_t),
        (to_ref, lambda i: rows_of(w_buf.at[1], rows, i)),
        (target_ref, lambda i: target_t),
    ]

    def swap(n):
        src, dst = swaps[n]

        @pl.when(p.kept)
        def _():
            pltpu.make_async_copy(src, dst(away), t_recv.at[n]).start()

        @pl.when(p.moved)
        def _():
            sends.start(
                lambda: (src, dst(away)),
                lambda: t_send.at[n],
                lambda: t_recv.at[n],
                lambda: p.dev(a=p.c, c=p.a),
                p.moved,
            )

    def swapped(n):
        wait_recv(swaps[n][1](home), t_recv.at[n])

    swap(0)

    share = tokens // xs

    def ho_rows(block, xx):
        return hob.at[block, pl.ds(pl.multiple_of(xx * share, 16), share)]

    @pl.when(p.kept)
    def _():
        sends.start(
            lambda: (
                ho_ref.at[pl.ds(pl.multiple_of(p.x * share, 16), share)],
                ho_rows(p.a, p.x),
            ),
            lambda: ho_send.at[0],
            lambda: ho_recv.at[0],
            lambda: p.dev(a=1 - p.a),
            p.kept,
        )

    swap(1)
    swap(2)
    swapped(0)
    ring_w = Ring(
        sends, p, w_buf.at[0], rows,
        (ring_send.at[0], ring_recv.at[0], pair_send.at[0], pair_recv.at[0]),
    )
    ring_q = Ring(
        sends, p, q_buf, depth,
        (ring_send.at[1], ring_recv.at[1], pair_send.at[1], pair_recv.at[1]),
    )
    ring_kv = Ring(
        sends, p, kv, tokens,
        (ring_send.at[2], ring_recv.at[2], pair_send.at[2], pair_recv.at[2]),
    )
    ring_t = Ring(
        sends, p, w_buf.at[1], rows,
        (ring_send.at[3], ring_recv.at[3], pair_send.at[3], pair_recv.at[3]),
        first,
    )
    ring_w.begin()

    @pl.when(p.moved)
    def _():
        wait_recv(ho_rows(p.c, p.x), ho_recv.at[0])
        for dx in range(1, xs):
            sends.same(
                lambda: ho_rows(p.c, p.x),
                lambda dx=dx: ho_send.at[dx],
                lambda dx=dx: ho_recv.at[dx],
                lambda dx=dx: p.dev(x=lax.rem(p.x + dx, xs)),
                p.moved,
            )

    swap(3)
    swap(4)
    swap(5)
    for k in range(1, steps):
        ring_w.advance(k)
    swapped(2)
    ring_q.begin()
    ring_w.advance(steps)
    own_ho.wait()

    @pl.when(p.moved)
    def _():
        for dx in range(1, xs):
            wait_recv(ho_rows(p.c, lax.rem(p.x + xs - dx, xs)), ho_recv.at[dx])
        sends.same(
            lambda: hob.at[p.c],
            lambda: ho_send.at[xs],
            lambda: ho_recv.at[xs],
            lambda: p.dev(c=1 - p.c),
            p.moved,
        )

    for k in range(steps + 1):
        ring_w.pair_arrived(k)
    swapped(1)

    wide = 2 * rows

    def project(lhs, which, out):
        def part(j, carry):
            at = pl.ds(pl.multiple_of(j * wide, 128), wide)
            out[...] += jnp.dot(
                lhs(j, at), w_buf[which, at, :], preferred_element_type=f32
            )
            return carry

        lax.fori_loop(0, inner // wide, part, 0)

    pred[...] = bi_t[...].astype(f32)
    project(lambda j, at: hob[p.c, :, at], 0, pred)

    @pl.when(first)
    def _():
        gen[...] = pred[...].astype(jnp.bfloat16)
        sends.start(
            lambda: (gen, gen_in), lambda: one_send.at[0], lambda: one_recv.at[0], lambda: p.dev(g=1), first
        )

    ring_q.advance(1)
    swapped(3)

    @pl.when(second)
    def _():
        wait_recv(gen_in, one_recv.at[0])
        gen[...] = gen_in[...]

    level = ts_ref[0].astype(f32) / 1000.0
    noisy[p.block] = (
        (1.0 - level) * gen[...].astype(f32) + level * noise_t[...].astype(f32)
    ).astype(jnp.bfloat16)

    def spread(buf, n, when=None):
        for rank, dx, da in p.fan():
            sends.same(
                lambda: buf.at[p.block],
                lambda rank=rank: fan_send.at[n, rank],
                lambda rank=rank: fan_recv.at[n, rank],
                lambda dx=dx, da=da: p.beside(dx, da),
                when,
            )

    def gathered(buf, n):
        for rank, dx, da in p.fan():
            block = 2 * lax.rem(p.x + xs - dx, xs) + lax.rem(p.a + da, 2)
            wait_recv(buf.at[block], fan_recv.at[n, rank])

    spread(noisy, 0)
    for k in range(2, steps):
        ring_q.advance(k)
    gathered(noisy, 0)

    def squares(f, total):
        block = noisy[f].astype(f32)
        return total + jnp.sum(block * block, axis=1, keepdims=True)

    total = lax.fori_loop(0, fans, squares, jnp.zeros((tokens, 1), f32))
    factor = lax.rsqrt(total * (1.0 / (fans * cols)) + norm_eps)

    def normalise(f, carry):
        norm[f] = (noisy[f].astype(f32) * factor).astype(jnp.bfloat16)
        return carry

    lax.fori_loop(0, fans, normalise, 0)
    for k in range(max(2, steps), steps + 1):
        ring_q.advance(k)
    for k in range(steps + 1):
        ring_q.pair_arrived(k)

    def head_norm(value):
        scale = lax.rsqrt(jnp.mean(value * value, axis=1, keepdims=True) + norm_eps)
        return (value * scale).astype(jnp.bfloat16)

    own_rows = pl.ds(pl.multiple_of(home * tokens, 16), tokens)

    def proj(n):
        value = jnp.zeros((tokens, local_inner), f32)
        for f in range(fans):
            value += jnp.dot(
                norm[f],
                q_buf[f * cols : (f + 1) * cols, n * local_inner : (n + 1) * local_inner],
                preferred_element_type=f32,
            )
        return value

    key_raw = proj(1)
    for h in range(heads):
        at = slice(h * HEAD_DIM, (h + 1) * HEAD_DIM)
        kv[own_rows, h * HEAD_DIM : (h + 1) * HEAD_DIM] = head_norm(key_raw[:, at])
    kv[own_rows, local_inner:] = proj(2).astype(jnp.bfloat16)
    ring_kv.begin()
    query_raw = proj(0)
    for h in range(heads):
        at = slice(h * HEAD_DIM, (h + 1) * HEAD_DIM)
        q_hat[:, at] = head_norm(query_raw[:, at])
    acc[...] = jnp.zeros_like(acc)
    lsum[...] = jnp.zeros_like(lsum)

    def attend(zz):
        at = pl.ds(pl.multiple_of(zz * 2 * tokens, 16), 2 * tokens)

        def one_head(h, carry):
            cut = pl.ds(pl.multiple_of(h * HEAD_DIM, HEAD_DIM), HEAD_DIM)
            cut_v = pl.ds(pl.multiple_of(local_inner + h * HEAD_DIM, HEAD_DIM), HEAD_DIM)
            scores = lax.dot_general(
                q_hat[:, cut], kv[at, cut], (((1,), (1,)), ((), ())), preferred_element_type=f32
            ) * (1.0 / math.sqrt(HEAD_DIM))
            weights = jnp.exp(scores)
            part = weights[:, :128]
            for j in range(1, 2 * tokens // 128):
                part += weights[:, j * 128 : (j + 1) * 128]
            lsum[h] += part
            acc[:, cut] += jnp.dot(
                weights.astype(jnp.bfloat16), kv[at, cut_v], preferred_element_type=f32
            )
            return carry

        lax.fori_loop(0, heads, one_head, 0)

    ring_kv.pair_arrived(0)
    attend(p.z)
    for k in range(1, steps + 1):
        ring_kv.advance(k)
        if k == steps:
            @pl.when(first)
            def _():
                swapped(4)
                ring_t.begin()
        if k > 1:
            ring_kv.pair_arrived(k - 1)
            for way in (0, 1):
                attend(ring_kv.zz(k - 1, way))
    ring_kv.pair_arrived(steps)
    attend(ring_kv.zz(steps, 0))

    for h in range(heads):
        at = slice(h * HEAD_DIM, (h + 1) * HEAD_DIM)
        att[p.block, :, at] = (
            acc[:, at] / jnp.sum(lsum[h], axis=1, keepdims=True)
        ).astype(jnp.bfloat16)
    spread(att, 1)

    @pl.when(first)
    def _():
        for k in range(1, steps + 1):
            ring_t.advance(k)
        for k in range(steps + 1):
            ring_t.pair_arrived(k)

    @pl.when(second)
    def _():
        swapped(4)

    gathered(att, 1)
    b_own[...] = jnp.zeros_like(b_own)
    project(lambda j, at: att[j], 1 - p.g, b_own)
    swapped(5)

    @pl.when(second)
    def _():
        sends.start(
            lambda: (b_own, b_in), lambda: one_send.at[1], lambda: one_recv.at[1], lambda: p.dev(g=0), second
        )
        grad[p.c] = (
            (pred[...] - target_t[...].astype(f32)) * (1.0 / math.sqrt(tokens * 2 * zs))
        ).astype(jnp.bfloat16)

    @pl.when(first)
    def _():
        guess = noisy[p.block].astype(f32) + b_own[...]
        gap = jnp.sum(jnp.abs(gen[...].astype(f32) - guess))
        gap_f[p.block] = jnp.full((8, 128), gap, f32)
        spread(gap_f, 2, first)
        wait_recv(b_in, one_recv.at[1])
        grad[p.c] = (b_in[...] - b_own[...]).astype(jnp.bfloat16)

    sends.same(
        lambda: grad.at[p.c], lambda: one_send.at[2], lambda: one_recv.at[2], lambda: p.dev(c=1 - p.c)
    )

    @pl.when(p.kept)
    def _():
        wait_recv(hob.at[1 - p.c], ho_recv.at[xs])

    wait_recv(grad.at[1 - p.c], one_recv.at[2])

    def partial(zz):
        at = pl.ds(pl.multiple_of(zz * wide, 128), wide)
        value = jnp.zeros((wide, cols), f32)
        for block in range(2):
            value += lax.dot_general(
                hob[block, :, at],
                grad[block],
                (((0,), (0,)), ((), ())),
                preferred_element_type=f32,
            )
        tmp[...] = value
        return tmp[pl.ds(pl.multiple_of(p.c * rows, 16), rows), :]

    def span(j, way):
        if j > 1:
            return slice(0, rows)
        return slice(0, rows // 2) if way == 0 else slice(rows // 2, rows)

    def rs_start(j, way):
        at = span(j, way)
        sends.start(
            lambda: (rs_send.at[j - 1, way, at], rs_recv.at[j - 1, way, at]),
            lambda: rs_ssem.at[j - 1, way],
            lambda: rs_rsem.at[j - 1, way],
            lambda: p.dev(z=p.zp if way == 0 else p.zm),
        )

    def rs_wait(j, way):
        wait_recv(rs_recv.at[j - 1, way, span(j, way)], rs_rsem.at[j - 1, way])

    def gap_step(j):
        if j == 1:
            gathered(gap_f, 2)
            gap_z[p.z] = jnp.sum(gap_f[...], axis=0)
            for dz in range(1, zs):
                sends.same(
                    lambda: gap_z.at[p.z],
                    lambda dz=dz: gz_send.at[dz],
                    lambda dz=dz: gz_recv.at[dz],
                    lambda dz=dz: p.dev(z=lax.rem(p.z + dz, zs)),
                    first,
                )
        if j == 2:
            for dz in range(1, zs):
                wait_recv(gap_z.at[lax.rem(p.z + zs - dz, zs)], gz_recv.at[dz])
            gap_c[p.c] = jnp.sum(gap_z[...], axis=0)
            sends.same(
                lambda: gap_c.at[p.c],
                lambda: one_send.at[3],
                lambda: one_recv.at[3],
                lambda: p.dev(c=1 - p.c),
                first,
            )
        if j == 3:
            wait_recv(gap_c.at[1 - p.c], one_recv.at[3])

    far = partial(lax.rem(p.z + steps, zs))
    for way in (0, 1):
        rs_send[0, way, span(1, way), :] = far[span(1, way)].astype(jnp.bfloat16)
        rs_start(1, way)
    pl.when(first)(lambda: gap_step(1))
    for j in range(2, steps + 1):
        for way in (0, 1):
            dist = steps - j + 1
            there = lax.rem(p.z + dist, zs) if way == 0 else lax.rem(p.z + zs - dist, zs)
            mine = partial(there)
            rs_wait(j - 1, way)
            at = span(j - 1, way)
            rs_send[j - 1, way] = mine.astype(jnp.bfloat16)
            rs_send[j - 1, way, at, :] = (
                mine[at] + rs_recv[j - 2, way, at, :].astype(f32)
            ).astype(jnp.bfloat16)
            rs_start(j, way)
        if j == 2:
            pl.when(first)(lambda: gap_step(2))
    if steps == 1:
        pl.when(first)(lambda: gap_step(2))
    mine = partial(p.z)
    pl.when(first)(lambda: gap_step(3))
    acc_w = tmp.at[0:rows]
    acc_w[...] = mine
    for way in (0, 1):
        rs_wait(steps, way)
        at = span(steps, way)
        acc_w[at, :] = acc_w[at, :] + rs_recv[steps - 1, way, at, :].astype(f32)

    @pl.when(first)
    def _():
        gap = (gap_c[0] + gap_c[1])[0:1, 0:1] * (1.0 / (tokens * 2 * zs * fans * cols))
        wg_out[...] = (acc_w[...] * (1.0 / (gap + norm_eps))).astype(jnp.bfloat16)

    @pl.when(second)
    def _():
        wg_out[...] = acc_w[...].astype(jnp.bfloat16)

    @pl.when(p.moved)
    def _():
        sends.start(
            lambda: (wg_out, wg_in),
            lambda: one_send.at[4],
            lambda: one_recv.at[4],
            lambda: p.dev(a=p.c, c=p.a),
            p.moved,
        )
        wait_recv(wg_in, one_recv.at[4])
        out_ref[...] = wg_in[...].astype(f32)

    @pl.when(p.kept)
    def _():
        out_ref[...] = wg_out[...].astype(f32)

    sends.finish()


def weight_gradient(zs, xs, ts, bi, ho, ww, qw, to, noise, target, interpret=None):
    tokens, inner = ho.shape
    cols = bi.shape[1]
    rows = ww.shape[0]
    depth, triple = qw.shape
    local_inner = triple // 3
    heads = local_inner // HEAD_DIM
    seq, fans, steps = 2 * zs, 2 * xs, zs // 2
    b16, f32 = jnp.bfloat16, jnp.float32
    vmem, dma = pltpu.VMEM, pltpu.SemaphoreType.DMA
    scratch = [
        vmem((2, inner, cols), b16),
        vmem((seq * depth, triple), b16),
        vmem((2, tokens, inner), b16),
        vmem((tokens, cols), b16),
        vmem((tokens, cols), b16),
        vmem((tokens, cols), b16),
        vmem((tokens, cols), b16),
        vmem((tokens, cols), b16),
        vmem((fans, tokens, cols), b16),
        vmem((fans, tokens, cols), b16),
        vmem((seq * tokens, 2 * local_inner), b16),
        vmem((tokens, local_inner), b16),
        vmem((tokens, local_inner), f32),
        vmem((heads, tokens, 128), f32),
        vmem((fans, tokens, local_inner), b16),
        vmem((tokens, cols), f32),
        vmem((tokens, cols), f32),
        vmem((tokens, cols), f32),
        vmem((2, tokens, cols), b16),
        vmem((2 * rows, cols), f32),
        vmem((steps, 2, rows, cols), b16),
        vmem((steps, 2, rows, cols), b16),
        vmem((fans, 8, 128), f32),
        vmem((zs, 8, 128), f32),
        vmem((2, 8, 128), f32),
        vmem((rows, cols), b16),
        vmem((rows, cols), b16),
        dma((6,)),
        dma((6,)),
        dma((xs + 1,)),
        dma((xs + 1,)),
        dma((4, steps, 2, 2)),
        dma((4, steps, 2, 2)),
        dma((4, steps + 1, 2, 2)),
        dma((4, steps + 1, 2, 2)),
        dma((3, fans)),
        dma((3, fans)),
        dma((steps, 2)),
        dma((steps, 2)),
        dma((zs,)),
        dma((zs,)),
        dma((5,)),
        dma((5,)),
        dma((1,)),
    ]
    in_vmem = pl.BlockSpec(memory_space=pltpu.VMEM)
    return pl.pallas_call(
        functools.partial(kernel, zs, xs),
        out_shape=jax.ShapeDtypeStruct((rows, cols), f32),
        in_specs=[pl.BlockSpec(memory_space=pltpu.SMEM), in_vmem, pl.BlockSpec(memory_space=pl.ANY)]
        + [in_vmem] * 5,
        out_specs=in_vmem,
        scratch_shapes=scratch,
        compiler_params=pltpu.CompilerParams(
            collective_id=0, has_side_effects=True, vmem_limit_bytes=56 * 1024 * 1024
        ),
        name="weight_gradient",
    )(ts, bi, ho, ww, qw, to, noise, target)


def body(
    block_input,
    head_outputs,
    out_master,
    first_moment,
    second_moment,
    score_qkv,
    teacher_out,
    noise,
    timestep,
    fake_target,
):
    zs, xs = lax.axis_size("seq") // 2, lax.axis_size("fsdp") // 2
    work_weight = out_master[0].astype(jnp.bfloat16)
    triple = score_qkv.shape[1] * score_qkv.shape[2]
    qw = score_qkv[0].reshape(triple, score_qkv.shape[3]).T
    weight_grad = weight_gradient(
        zs, xs, timestep, block_input[0], head_outputs[0], work_weight, qw, teacher_out, noise,
        fake_target,
    )
    new_first = 0.9 * first_moment[0] + 0.1 * weight_grad
    new_second = 0.95 * second_moment[0] + 0.05 * weight_grad * weight_grad
    new_master = out_master[0] - learn_rate * (new_first / first_fix) / (
        jnp.sqrt(new_second / second_fix) + 1e-08
    )
    return (new_master[None], new_first[None], new_second[None])


def solution(mesh):
    placed = (
        P("group", "seq", "fsdp"),
        P("group", "seq", None),
        P("group", "seq", "fsdp"),
        P("group", "seq", "fsdp"),
        P("group", "seq", "fsdp"),
        P("group", None, "fsdp", "seq"),
        P("seq", "fsdp"),
        P("seq", "fsdp"),
        P(),
        P("seq", "fsdp"),
    )
    return jax.shard_map(
        body,
        mesh=mesh,
        in_specs=placed,
        out_specs=(P("group", "seq", "fsdp"), P("group", "seq", "fsdp"), P("group", "seq", "fsdp")),
        check_vma=False,
    )
```

time: 1120 us -> 186 us (0.17)
  waiting for transfers between devices: 687 us -> 0 us
  blocking collectives: 324 us -> 0 us
  Pallas kernels: 0 us -> 177 us
  matrix products: 36.3 us -> 0 us
  local copies, waits for them, and re-layouts: 40.4 us -> 4.57 us
  between operations: 15.6 us -> 1.41 us
    all_gather x7 -> x0, waiting for transfers between devices: 472 us -> none  [the longest x1 111 us: body(): lax.all_gather(score_qkv[0], 'seq', axis=2, tiled=True)]
    psum x1 -> x0, blocking collectives: 324 us -> none  [body(): lax.psum(jnp.sum(jnp.abs(source.astype(jnp.float32) - teacher_guess)), ('...]
    reduce_scatter x1 -> x0, waiting for transfers between devices: 212 us -> none  [body(): lax.psum_scatter(lax.dot_general(own_heads, grad_rows, (((0,), (0,)), (()...]
    pallas_call x0 -> x1, Pallas kernels: none -> 177 us  [weight_gradient(): pl.pallas_call(functools.partial(kernel, zs, xs), out_shape=jax.ShapeDtyp...]
    dot_general x20 -> x0, matrix products: 36.3 us -> none  [the longest x8 11.8 us: attend_block(): jnp.einsum('qhd,khd->hqk', query_shaped, key_shaped, preferred_element_ty...]
    reshape x2 -> x0, local copies, waits for them, and re-layouts: 18 us -> none  [the longest x1 9 us: body(): value_piece.reshape(key_count // block_size, block_size, local_heads, HEA...]
    unnamed x24 -> x17, local copies, waits for them, and re-layouts: 18.5 us -> 4.57 us
  transfers between devices with their start and end apart: 10 -> 0, of which waited for: 9 -> 0; matrix products, arithmetic and copies ran while one was open for 5% -> 0% of each run, Pallas kernels for 0% -> 0%
where the time goes in v1:
time: 186 us
  Pallas kernels  177 us (95%)
  local copies, waits for them, and re-layouts  4.57 us (2%)
  other arithmetic  2.74 us (1%)
    pallas_call x1, Pallas kernels, weight_gradient(): pl.pallas_call(functools.partial(kernel, zs, xs), out_shape=jax.ShapeDtyp...  177 us
    unnamed x17, local copies, waits for them, and re-layouts  4.57 us

profile of v1, /device:TPU:1, one launch (start us, length us, event | category | flops | bytes accessed | tf_op | source)
XLA Modules:
  0.0 185.7 jit_solution(8470060070901469468)
XLA Ops:
  0.6 0.0 copy-start.3
  0.6 0.0 copy-start.4
  0.7 0.0 copy-start.5
  0.7 0.0 copy-start
  0.7 1.3 copy.18
  2.0 0.8 copy.21
  2.8 0.0 copy-done.3
  2.8 0.8 copy.17
  3.6 0.0 copy-done.4
  3.6 0.8 copy.19.noise_ref
  4.4 0.0 copy-done.5
  4.4 0.8 copy.20.target_ref
  5.2 0.0 copy-done
  5.2 0.7 bitcast_convert_fusion.ww_ref
  5.9 0.0 copy-start.1
  5.9 0.0 copy-start.2
  6.6 177.0 %weight_gradient.1 = f32[192,320]{1,0:T(8,128)} custom-call(s32[1]{0:T(128)S(6)} %copy.22.ts_ref, bf16[256,320]{1,0:T(8,128)(2,1)} %bitcast.35, bf16[256,3072]{1,0:T(8,128)(2,1)} %bitcast.33, bf16[192,320]{1,0:T(8,128)(2,1)} %bitcast_convert_fusion.ww_ref, bf16[160,1152]{1,0:T(8,128)(2,1)} %bitcast.34, bf16[192,320]{1,0:T(8,128)(2,1)} %to_ref.1, ...), custom_call_target="tpu_custom_call" | custom-call | tf_op jit(solution)/shard_map/weight_gradient/pallas_call | solution.py:707
  183.6 0.0 copy-done.1
  183.6 0.0 copy-done.2
  183.6 2.1 %fusion.3 = (f32[1,192,320]{2,1,0:T(8,128)}, f32[1,192,320]{2,1,0:T(8,128)}, f32[1,192,320]{2,1,0:T(8,128)}) fusion(f32[192,320]{1,0:T(8,128)} %weight_gradient.1, f32[1,192,320]{2,1,0:T(8,128)S(1)} %copy-done.1, f32[1,192,320]{2,1,0:T(8,128)S(1)} %copy-done.2, f32[1,192,320]{2,1,0:T(8,128)S(1)} %copy-done), kind=kLoop, calls=%fused_computation.7 | loop fusion | flops 737280 | bytes 1720320 | tf_op jit(solution)/shard_map/broadcast_in_dim | solution.py:746
Async XLA Ops:
  0.6 2.1 %copy-start.3 = (bf16[1,256,320]{1,2,0:T(8,128)(2,1)S(1)}, bf16[1,256,320]{1,2,0:T(8,128)(2,1)}, u32[]{:S(2)}) copy-start(bf16[1,256,320]{1,2,0:T(8,128)(2,1)} %param.10) | copy-start | bytes 491524
  0.6 3.0 %copy-start.4 = (bf16[256,320]{0,1:T(8,128)(2,1)S(1)}, bf16[256,320]{0,1:T(8,128)(2,1)}, u32[]{:S(2)}) copy-start(bf16[256,320]{0,1:T(8,128)(2,1)} %param.17) | copy-start | bytes 491524
  0.7 3.8 %copy-start.5 = (bf16[256,320]{0,1:T(8,128)(2,1)S(1)}, bf16[256,320]{0,1:T(8,128)(2,1)}, u32[]{:S(2)}) copy-start(bf16[256,320]{0,1:T(8,128)(2,1)} %param.19) | copy-start | bytes 491524
  0.7 4.6 %copy-start = (f32[1,192,320]{2,1,0:T(8,128)S(1)}, f32[1,192,320]{2,1,0:T(8,128)}, u32[]{:S(2)}) copy-start(f32[1,192,320]{2,1,0:T(8,128)} %param.12) | copy-start | bytes 737284
  5.9 177.7 %copy-start.1 = (f32[1,192,320]{2,1,0:T(8,128)S(1)}, f32[1,192,320]{2,1,0:T(8,128)}, u32[]{:S(2)}) copy-start(f32[1,192,320]{2,1,0:T(8,128)} %param.14) | copy-start | bytes 737284
  5.9 177.7 %copy-start.2 = (f32[1,192,320]{2,1,0:T(8,128)S(1)}, f32[1,192,320]{2,1,0:T(8,128)}, u32[]{:S(2)}) copy-start(f32[1,192,320]{2,1,0:T(8,128)} %param.13) | copy-start | bytes 737284

commit v2 on v1

--- a/solution.py
+++ b/solution.py
@@ -58,12 +58,16 @@
 
 
 class Ring:
-    def __init__(self, sends, place, buf, rows, sems, when=None):
+    def __init__(self, sends, place, buf, rows, sems, when=None, split=False):
         self.sends, self.place, self.buf, self.rows, self.when = sends, place, buf, rows, when
+        self.split = split
         self.ring_send, self.ring_recv, self.pair_send, self.pair_recv = sems
         self.steps = place.zs // 2
 
     def piece(self, zz, cc, half):
+        if self.split:
+            start = (2 * zz + cc) * self.rows
+            return self.buf.at[half, pl.ds(pl.multiple_of(start, 16), self.rows)]
         each = self.rows // 2
         start = (2 * zz + cc) * self.rows + half * each
         return self.buf.at[pl.ds(pl.multiple_of(start, 16), each)]
@@ -97,10 +101,11 @@
             self.when,
         )
 
-    def begin(self):
+    def begin(self, halves=(0, 1)):
         for way, half in self.parts(1):
-            self.send(1, way, half)
-        for half in (0, 1):
+            if half in halves:
+                self.send(1, way, half)
+        for half in halves:
             self.pair(0, 0, half)
 
     def advance(self, k):
@@ -119,6 +124,66 @@
                 self.piece(self.zz(k, way), 1 - self.place.c, half),
                 self.pair_recv.at[k, way, half],
             )
+
+
+class Across:
+    def __init__(self, sends, place, buf, sems):
+        self.sends, self.place, self.buf = sends, place, buf
+        self.send_sem, self.recv_sem = sems
+        self.rows = buf.shape[1]
+
+    def part(self, dx, other, half, quarter=None):
+        p = self.place
+        block = 2 * lax.rem(p.x + dx + p.xs, p.xs) + (1 - p.a if other else p.a)
+        each = self.rows // 2
+        start = half * each
+        if quarter is not None:
+            each = each // 2
+            start = start + quarter * each
+        return self.buf.at[block, pl.ds(start, each)]
+
+    def go(self, n, ref, device):
+        self.sends.same(ref, lambda: self.send_sem.at[n], lambda: self.recv_sem.at[n], device)
+
+    def beside(self, way):
+        p = self.place
+        return p.dev(x=lax.rem(p.x + (1 if way == 0 else p.xs - 1), p.xs))
+
+    def cross(self, half):
+        p = self.place
+        self.go(half, lambda: self.part(0, False, half), lambda: p.dev(a=1 - p.a))
+
+    def crossed(self, half):
+        wait_recv(self.part(0, True, half), self.recv_sem.at[half])
+
+    def step(self, other, half):
+        for way in (0, 1):
+            self.go(
+                2 + 4 * other + 2 * half + way,
+                lambda: self.part(0, other, half),
+                lambda way=way: self.beside(way),
+            )
+
+    def forward(self, other, half):
+        for way in (0, 1):
+            near = -1 if way == 0 else 1
+            n = 4 * other + 2 * half + way
+            wait_recv(self.part(near, other, half), self.recv_sem.at[2 + n])
+            self.go(
+                10 + n,
+                lambda near=near, way=way: self.part(near, other, half, way),
+                lambda way=way: self.beside(way),
+            )
+
+    def arrived(self, half):
+        for other in (0, 1):
+            for way in (0, 1):
+                n = 4 * other + 2 * half + way
+                wait_recv(self.part(2, other, half, way), self.recv_sem.at[10 + n])
+
+    def begin(self, half):
+        self.cross(half)
+        self.step(0, half)
 
 
 class Place:
@@ -133,6 +198,8 @@
         self.block = 2 * self.x + self.a
         self.kept = self.a == self.c
         self.moved = self.a != self.c
+        self.first = self.g == 0
+        self.second = self.g == 1
 
     def dev(self, g=None, z=None, a=None, x=None, c=None):
         g = self.g if g is None else g
@@ -200,6 +267,8 @@
     fan_recv,
     rs_ssem,
     rs_rsem,
+    gf_send,
+    gf_recv,
     gz_send,
     gz_recv,
     one_send,
@@ -216,8 +285,8 @@
     heads = local_inner // HEAD_DIM
     steps = zs // 2
     fans = 2 * xs
-    first = p.g == 0
-    second = p.g == 1
+    first = p.first
+    second = p.second
     f32 = jnp.float32
 
     barrier = pltpu.get_barrier_semaphore()
@@ -242,9 +311,10 @@
         (noise_ref, lambda i: noise_t),
         (to_ref, lambda i: rows_of(w_buf.at[1], rows, i)),
         (target_ref, lambda i: target_t),
+        (ww_ref, lambda i: rows_of(w_buf.at[1], rows, i)),
     ]
 
-    def swap(n):
+    def swap(n, when):
         src, dst = swaps[n]
 
         @pl.when(p.kept)
@@ -258,91 +328,92 @@
                 lambda: t_send.at[n],
                 lambda: t_recv.at[n],
                 lambda: p.dev(a=p.c, c=p.a),
-                p.moved,
-            )
+                when,
+            )
+
+    first_moved, second_moved = first & p.moved, second & p.moved
+    first_kept, second_kept = first & p.kept, second & p.kept
 
     def swapped(n):
         wait_recv(swaps[n][1](home), t_recv.at[n])
 
-    swap(0)
-
     share = tokens // xs
 
-    def ho_rows(block, xx):
-        return hob.at[block, pl.ds(pl.multiple_of(xx * share, 16), share)]
-
-    @pl.when(p.kept)
-    def _():
-        sends.start(
-            lambda: (
-                ho_ref.at[pl.ds(pl.multiple_of(p.x * share, 16), share)],
-                ho_rows(p.a, p.x),
-            ),
-            lambda: ho_send.at[0],
-            lambda: ho_recv.at[0],
-            lambda: p.dev(a=1 - p.a),
-            p.kept,
-        )
-
-    swap(1)
-    swap(2)
-    swapped(0)
-    ring_w = Ring(
-        sends, p, w_buf.at[0], rows,
-        (ring_send.at[0], ring_recv.at[0], pair_send.at[0], pair_recv.at[0]),
-    )
-    ring_q = Ring(
-        sends, p, q_buf, depth,
-        (ring_send.at[1], ring_recv.at[1], pair_send.at[1], pair_recv.at[1]),
-    )
-    ring_kv = Ring(
-        sends, p, kv, tokens,
-        (ring_send.at[2], ring_recv.at[2], pair_send.at[2], pair_recv.at[2]),
-    )
-    ring_t = Ring(
-        sends, p, w_buf.at[1], rows,
-        (ring_send.at[3], ring_recv.at[3], pair_send.at[3], pair_recv.at[3]),
-        first,
-    )
-    ring_w.begin()
-
-    @pl.when(p.moved)
-    def _():
-        wait_recv(ho_rows(p.c, p.x), ho_recv.at[0])
-        for dx in range(1, xs):
+    def ho_rows(block, dx, half=None):
+        start = lax.rem(p.x + dx + xs, xs) * share
+        each = share
+        if half is not None:
+            each = share // 2
+            start = start + half * each
+        return hob.at[block, pl.ds(pl.multiple_of(start, 16), each)]
+
+    def ho_cross(when):
+        @pl.when(p.kept)
+        def _():
+            sends.start(
+                lambda: (
+                    ho_ref.at[pl.ds(pl.multiple_of(p.x * share, 16), share)],
+                    ho_rows(p.a, 0),
+                ),
+                lambda: ho_send.at[0],
+                lambda: ho_recv.at[0],
+                lambda: p.dev(a=1 - p.a),
+                when,
+            )
+
+    def beside(way):
+        return p.dev(x=lax.rem(p.x + (1 if way == 0 else xs - 1), xs))
+
+    def ho_step(when):
+        @pl.when(p.moved)
+        def _():
+            wait_recv(ho_rows(p.c, 0), ho_recv.at[0])
+            for way in (0, 1):
+                sends.same(
+                    lambda: ho_rows(p.c, 0),
+                    lambda way=way: ho_send.at[1 + way],
+                    lambda way=way: ho_recv.at[1 + way],
+                    lambda way=way: beside(way),
+                    when,
+                )
+
+    def ho_forward(when):
+        @pl.when(p.moved)
+        def _():
+            for way in (0, 1):
+                near = -1 if way == 0 else 1
+                wait_recv(ho_rows(p.c, near), ho_recv.at[1 + way])
+                sends.same(
+                    lambda near=near, way=way: ho_rows(p.c, near, way),
+                    lambda way=way: ho_send.at[3 + way],
+                    lambda way=way: ho_recv.at[3 + way],
+                    lambda way=way: beside(way),
+                    when,
+                )
+
+    def ho_arrived(when):
+        @pl.when(p.moved)
+        def _():
+            for way in (0, 1):
+                wait_recv(ho_rows(p.c, 2, way), ho_recv.at[3 + way])
             sends.same(
-                lambda: ho_rows(p.c, p.x),
-                lambda dx=dx: ho_send.at[dx],
-                lambda dx=dx: ho_recv.at[dx],
-                lambda dx=dx: p.dev(x=lax.rem(p.x + dx, xs)),
-                p.moved,
-            )
-
-    swap(3)
-    swap(4)
-    swap(5)
-    for k in range(1, steps):
-        ring_w.advance(k)
-    swapped(2)
-    ring_q.begin()
-    ring_w.advance(steps)
-    own_ho.wait()
-
-    @pl.when(p.moved)
-    def _():
-        for dx in range(1, xs):
-            wait_recv(ho_rows(p.c, lax.rem(p.x + xs - dx, xs)), ho_recv.at[dx])
-        sends.same(
-            lambda: hob.at[p.c],
-            lambda: ho_send.at[xs],
-            lambda: ho_recv.at[xs],
-            lambda: p.dev(c=1 - p.c),
-            p.moved,
-        )
-
-    for k in range(steps + 1):
-        ring_w.pair_arrived(k)
-    swapped(1)
+                lambda: hob.at[p.c],
+                lambda: ho_send.at[5],
+                lambda: ho_recv.at[5],
+                lambda: p.dev(c=1 - p.c),
+                when,
+            )
+
+    def ring(buf, each, n, when=None, split=False):
+        sems = (ring_send.at[n], ring_recv.at[n], pair_send.at[n], pair_recv.at[n])
+        return Ring(sends, p, buf, each, sems, when, split)
+
+    ring_w = ring(w_buf.at[0], rows, 0, first)
+    ring_qs = [ring(q_buf, depth, 1, first), ring(q_buf, depth, 1, second)]
+    ring_kv = ring(kv, tokens, 2, split=True)
+    ring_t = ring(w_buf.at[1], rows, 3)
+    over_noisy = Across(sends, p, noisy, (fan_send.at[0], fan_recv.at[0]))
+    over_att = Across(sends, p, att, (fan_send.at[1], fan_recv.at[1]))
 
     wide = 2 * rows
 
@@ -356,48 +427,116 @@
 
         lax.fori_loop(0, inner // wide, part, 0)
 
-    pred[...] = bi_t[...].astype(f32)
-    project(lambda j, at: hob[p.c, :, at], 0, pred)
+    def gap_spread():
+        for rank, dx, da in p.fan():
+            sends.same(
+                lambda: gap_f.at[p.block],
+                lambda rank=rank: gf_send.at[rank],
+                lambda rank=rank: gf_recv.at[rank],
+                lambda dx=dx, da=da: p.beside(dx, da),
+                first,
+            )
+
+    def gap_gathered():
+        for rank, dx, da in p.fan():
+            block = 2 * lax.rem(p.x + xs - dx, xs) + lax.rem(p.a + da, 2)
+            wait_recv(gap_f.at[block], gf_recv.at[rank])
+
+    def predict(which):
+        pred[...] = bi_t[...].astype(f32)
+        project(lambda j, at: hob[p.c, :, at], which, pred)
+
+    half_rows = [slice(0, tokens // 2), slice(tokens // 2, tokens)]
 
     @pl.when(first)
     def _():
+        ring_q = ring_qs[0]
+        swap(0, first_moved)
+        ho_cross(first_kept)
+        swap(1, first_moved)
+        swapped(0)
+        ring_w.begin()
+        swap(3, first_moved)
+        swap(2, first_moved)
+        ring_w.advance(1)
+        ho_step(first_moved)
+        ring_w.advance(2)
+        ring_w.advance(3)
+        ho_forward(first_moved)
+        swapped(2)
+        ring_q.begin()
+        swap(4, first_moved)
+        ring_w.advance(4)
+        own_ho.wait()
+        ho_arrived(first_moved)
+        for k in range(steps + 1):
+            ring_w.pair_arrived(k)
+        swapped(1)
+        predict(0)
         gen[...] = pred[...].astype(jnp.bfloat16)
-        sends.start(
-            lambda: (gen, gen_in), lambda: one_send.at[0], lambda: one_recv.at[0], lambda: p.dev(g=1), first
-        )
-
-    ring_q.advance(1)
-    swapped(3)
+        for h in (0, 1):
+            sends.start(
+                lambda h=h: (gen.at[half_rows[h]], gen_in.at[half_rows[h]]),
+                lambda h=h: one_send.at[h],
+                lambda h=h: one_recv.at[h],
+                lambda: p.dev(g=1),
+                first,
+            )
 
     @pl.when(second)
     def _():
-        wait_recv(gen_in, one_recv.at[0])
-        gen[...] = gen_in[...]
-
+        ring_q = ring_qs[1]
+        swap(2, second_moved)
+        swapped(2)
+        ring_q.begin()
+        swap(3, second_moved)
+        ring_q.advance(1)
+        swap(6, second_moved)
+        ring_q.advance(2)
+        ho_cross(second_kept)
+        swap(1, second_moved)
+        ring_q.advance(3)
+        ho_step(second_moved)
+        swap(5, second_moved)
+        ring_q.advance(4)
+        ho_forward(second_moved)
+        own_ho.wait()
+
+    swapped(3)
     level = ts_ref[0].astype(f32) / 1000.0
-    noisy[p.block] = (
-        (1.0 - level) * gen[...].astype(f32) + level * noise_t[...].astype(f32)
-    ).astype(jnp.bfloat16)
-
-    def spread(buf, n, when=None):
-        for rank, dx, da in p.fan():
-            sends.same(
-                lambda: buf.at[p.block],
-                lambda rank=rank: fan_send.at[n, rank],
-                lambda rank=rank: fan_recv.at[n, rank],
-                lambda dx=dx, da=da: p.beside(dx, da),
-                when,
-            )
-
-    def gathered(buf, n):
-        for rank, dx, da in p.fan():
-            block = 2 * lax.rem(p.x + xs - dx, xs) + lax.rem(p.a + da, 2)
-            wait_recv(buf.at[block], fan_recv.at[n, rank])
-
-    spread(noisy, 0)
-    for k in range(2, steps):
-        ring_q.advance(k)
-    gathered(noisy, 0)
+    for h in (0, 1):
+        at = half_rows[h]
+
+        @pl.when(second)
+        def _():
+            wait_recv(gen_in.at[at], one_recv.at[h])
+            gen[at, :] = gen_in[at, :]
+
+        noisy[p.block, at, :] = (
+            (1.0 - level) * gen[at, :].astype(f32) + level * noise_t[at, :].astype(f32)
+        ).astype(jnp.bfloat16)
+        over_noisy.begin(h)
+
+    def first_q(k):
+        pl.when(first)(lambda: ring_qs[0].advance(k))
+
+    over_noisy.forward(0, 0)
+    first_q(1)
+    over_noisy.crossed(0)
+    over_noisy.step(1, 0)
+    over_noisy.forward(0, 1)
+    over_noisy.crossed(1)
+    over_noisy.step(1, 1)
+    first_q(2)
+    over_noisy.forward(1, 0)
+    over_noisy.forward(1, 1)
+    first_q(3)
+    over_noisy.arrived(0)
+    over_noisy.arrived(1)
+
+    @pl.when(second)
+    def _():
+        ho_arrived(second_moved)
 
     def squares(f, total):
         block = noisy[f].astype(f32)
@@ -411,10 +550,9 @@
         return carry
 
     lax.fori_loop(0, fans, normalise, 0)
-    for k in range(max(2, steps), steps + 1):
-        ring_q.advance(k)
+    first_q(4)
     for k in range(steps + 1):
-        ring_q.pair_arrived(k)
+        ring_qs[0].pair_arrived(k)
 
     def head_norm(value):
         scale = lax.rsqrt(jnp.mean(value * value, axis=1, keepdims=True) + norm_eps)
@@ -435,9 +573,10 @@
     key_raw = proj(1)
     for h in range(heads):
         at = slice(h * HEAD_DIM, (h + 1) * HEAD_DIM)
-        kv[own_rows, h * HEAD_DIM : (h + 1) * HEAD_DIM] = head_norm(key_raw[:, at])
-    kv[own_rows, local_inner:] = proj(2).astype(jnp.bfloat16)
-    ring_kv.begin()
+        kv[0, own_rows, at] = head_norm(key_raw[:, at])
+    ring_kv.begin((0,))
+    kv[1, own_rows, :] = proj(2).astype(jnp.bfloat16)
+    ring_kv.begin((1,))
     query_raw = proj(0)
     for h in range(heads):
         at = slice(h * HEAD_DIM, (h + 1) * HEAD_DIM)
@@ -450,9 +589,8 @@
 
         def one_head(h, carry):
             cut = pl.ds(pl.multiple_of(h * HEAD_DIM, HEAD_DIM), HEAD_DIM)
-            cut_v = pl.ds(pl.multiple_of(local_inner + h * HEAD_DIM, HEAD_DIM), HEAD_DIM)
             scores = lax.dot_general(
-                q_hat[:, cut], kv[at, cut], (((1,), (1,)), ((), ())), preferred_element_type=f32
+                q_hat[:, cut], kv[0, at, cut], (((1,), (1,)), ((), ())), preferred_element_type=f32
             ) * (1.0 / math.sqrt(HEAD_DIM))
             weights = jnp.exp(scores)
             part = weights[:, :128]
@@ -460,7 +598,7 @@
                 part += weights[:, j * 128 : (j + 1) * 128]
             lsum[h] += part
             acc[:, cut] += jnp.dot(
-                weights.astype(jnp.bfloat16), kv[at, cut_v], preferred_element_type=f32
+                weights.astype(jnp.bfloat16), kv[1, at, cut], preferred_element_type=f32
             )
             return carry
 
@@ -471,10 +609,9 @@
     for k in range(1, steps + 1):
         ring_kv.advance(k)
         if k == steps:
-            @pl.when(first)
-            def _():
-                swapped(4)
-                ring_t.begin()
+            pl.when(first)(lambda: swapped(4))
+            pl.when(second)(lambda: swapped(6))
+            ring_t.begin()
         if k > 1:
             ring_kv.pair_arrived(k - 1)
             for way in (0, 1):
@@ -482,34 +619,63 @@
     ring_kv.pair_arrived(steps)
     attend(ring_kv.zz(steps, 0))
 
-    for h in range(heads):
-        at = slice(h * HEAD_DIM, (h + 1) * HEAD_DIM)
-        att[p.block, :, at] = (
-            acc[:, at] / jnp.sum(lsum[h], axis=1, keepdims=True)
-        ).astype(jnp.bfloat16)
-    spread(att, 1)
-
-    @pl.when(first)
-    def _():
-        for k in range(1, steps + 1):
-            ring_t.advance(k)
-        for k in range(steps + 1):
-            ring_t.pair_arrived(k)
+    for half in (0, 1):
+        rr = half_rows[half]
+        for h in range(heads):
+            at = slice(h * HEAD_DIM, (h + 1) * HEAD_DIM)
+            att[p.block, rr, at] = (
+                acc[rr, at] / jnp.sum(lsum[h, rr, :], axis=1, keepdims=True)
+            ).astype(jnp.bfloat16)
+        over_att.begin(half)
+    over_att.forward(0, 0)
+    ring_t.advance(1)
+    over_att.crossed(0)
+    over_att.step(1, 0)
+    over_att.forward(0, 1)
+    ring_t.advance(2)
+    over_att.crossed(1)
+    over_att.step(1, 1)
+    over_att.forward(1, 0)
+    ring_t.advance(3)
+    over_att.forward(1, 1)
+    ring_t.advance(4)
+    for k in range(steps + 1):
+        ring_t.pair_arrived(k)
+
+    def pass_branch(h):
+        sends.start(
+            lambda: (b_own.at[half_rows[h]], b_in.at[half_rows[h]]),
+            lambda: one_send.at[2 + h],
+            lambda: one_recv.at[2 + h],
+            lambda: p.dev(g=0),
+            second,
+        )
+
+    for h in (0, 1):
+        rr = half_rows[h]
+        over_att.arrived(h)
+        value = jnp.zeros((tokens // 2, cols), f32)
+        for j in range(fans):
+            value += jnp.dot(
+                att[j, rr, :], w_buf[1, j * wide : (j + 1) * wide, :], preferred_element_type=f32
+            )
+        b_own[rr, :] = value
+
+        pl.when(second)(lambda: pass_branch(h))
+
+    def pass_grad(h):
+        sends.same(
+            lambda h=h: grad.at[p.c, half_rows[h]],
+            lambda: one_send.at[4 + h],
+            lambda: one_recv.at[4 + h],
+            lambda: p.dev(c=1 - p.c),
+        )
 
     @pl.when(second)
     def _():
-        swapped(4)
-
-    gathered(att, 1)
-    b_own[...] = jnp.zeros_like(b_own)
-    project(lambda j, at: att[j], 1 - p.g, b_own)
-    swapped(5)
-
-    @pl.when(second)
-    def _():
-        sends.start(
-            lambda: (b_own, b_in), lambda: one_send.at[1], lambda: one_recv.at[1], lambda: p.dev(g=0), second
-        )
+        swapped(1)
+        swapped(5)
+        predict(1)
         grad[p.c] = (
             (pred[...] - target_t[...].astype(f32)) * (1.0 / math.sqrt(tokens * 2 * zs))
         ).astype(jnp.bfloat16)
@@ -519,19 +685,24 @@
         guess = noisy[p.block].astype(f32) + b_own[...]
         gap = jnp.sum(jnp.abs(gen[...].astype(f32) - guess))
         gap_f[p.block] = jnp.full((8, 128), gap, f32)
-        spread(gap_f, 2, first)
-        wait_recv(b_in, one_recv.at[1])
-        grad[p.c] = (b_in[...] - b_own[...]).astype(jnp.bfloat16)
-
-    sends.same(
-        lambda: grad.at[p.c], lambda: one_send.at[2], lambda: one_recv.at[2], lambda: p.dev(c=1 - p.c)
-    )
+        gap_spread()
+
+    for h in (0, 1):
+        rr = half_rows[h]
+
+        @pl.when(first)
+        def _():
+            wait_recv(b_in.at[rr], one_recv.at[2 + h])
+            grad[p.c, rr, :] = (b_in[rr, :] - b_own[rr, :]).astype(jnp.bfloat16)
+
+        pass_grad(h)
 
     @pl.when(p.kept)
     def _():
-        wait_recv(hob.at[1 - p.c], ho_recv.at[xs])
-
-    wait_recv(grad.at[1 - p.c], one_recv.at[2])
+        wait_recv(hob.at[1 - p.c], ho_recv.at[5])
+
+    for h in (0, 1):
+        wait_recv(grad.at[1 - p.c, half_rows[h]], one_recv.at[4 + h])
 
     def partial(zz):
         at = pl.ds(pl.multiple_of(zz * wide, 128), wide)
@@ -565,7 +736,7 @@
 
     def gap_step(j):
         if j == 1:
-            gathered(gap_f, 2)
+            gap_gathered()
             gap_z[p.z] = jnp.sum(gap_f[...], axis=0)
             for dz in range(1, zs):
                 sends.same(
@@ -581,13 +752,13 @@
             gap_c[p.c] = jnp.sum(gap_z[...], axis=0)
             sends.same(
                 lambda: gap_c.at[p.c],
-                lambda: one_send.at[3],
-                lambda: one_recv.at[3],
+                lambda: one_send.at[6],
+                lambda: one_recv.at[6],
                 lambda: p.dev(c=1 - p.c),
                 first,
             )
         if j == 3:
-            wait_recv(gap_c.at[1 - p.c], one_recv.at[3])
+            wait_recv(gap_c.at[1 - p.c], one_recv.at[6])
 
     far = partial(lax.rem(p.z + steps, zs))
     for way in (0, 1):
@@ -632,12 +803,12 @@
     def _():
         sends.start(
             lambda: (wg_out, wg_in),
-            lambda: one_send.at[4],
-            lambda: one_recv.at[4],
+            lambda: one_send.at[7],
+            lambda: one_recv.at[7],
             lambda: p.dev(a=p.c, c=p.a),
             p.moved,
         )
-        wait_recv(wg_in, one_recv.at[4])
+        wait_recv(wg_in, one_recv.at[7])
         out_ref[...] = wg_in[...].astype(f32)
 
     @pl.when(p.kept)
@@ -668,7 +839,7 @@
         vmem((tokens, cols), b16),
         vmem((fans, tokens, cols), b16),
         vmem((fans, tokens, cols), b16),
-        vmem((seq * tokens, 2 * local_inner), b16),
+        vmem((2, seq * tokens, local_inner), b16),
         vmem((tokens, local_inner), b16),
         vmem((tokens, local_inner), f32),
         vmem((heads, tokens, 128), f32),
@@ -685,34 +856,35 @@
         vmem((2, 8, 128), f32),
         vmem((rows, cols), b16),
         vmem((rows, cols), b16),
+        dma((7,)),
+        dma((7,)),
         dma((6,)),
         dma((6,)),
-        dma((xs + 1,)),
-        dma((xs + 1,)),
         dma((4, steps, 2, 2)),
         dma((4, steps, 2, 2)),
         dma((4, steps + 1, 2, 2)),
         dma((4, steps + 1, 2, 2)),
-        dma((3, fans)),
-        dma((3, fans)),
+        dma((2, 18)),
+        dma((2, 18)),
         dma((steps, 2)),
         dma((steps, 2)),
+        dma((fans,)),
+        dma((fans,)),
         dma((zs,)),
         dma((zs,)),
-        dma((5,)),
-        dma((5,)),
+        dma((8,)),
+        dma((8,)),
         dma((1,)),
     ]
     in_vmem = pl.BlockSpec(memory_space=pltpu.VMEM)
     return pl.pallas_call(
         functools.partial(kernel, zs, xs),
         out_shape=jax.ShapeDtypeStruct((rows, cols), f32),
-        in_specs=[pl.BlockSpec(memory_space=pltpu.SMEM), in_vmem, pl.BlockSpec(memory_space=pl.ANY)]
-        + [in_vmem] * 5,
+        in_specs=[pl.BlockSpec(memory_space=pltpu.SMEM)] + [pl.BlockSpec(memory_space=pl.ANY)] * 7,
         out_specs=in_vmem,
         scratch_shapes=scratch,
         compiler_params=pltpu.CompilerParams(
-            collective_id=0, has_side_effects=True, vmem_limit_bytes=56 * 1024 * 1024
+            collective_id=0, has_side_effects=True, vmem_limit_bytes=62 * 1024 * 1024
         ),
         name="weight_gradient",
     )(ts, bi, ho, ww, qw, to, noise, target)

time: 186 us -> 175 us (0.941)
  Pallas kernels: 177 us -> 166 us
    pallas_call x1, Pallas kernels: 177 us -> 166 us  [weight_gradient(): pl.pallas_call(functools.partial(kernel, zs, xs), out_shape=jax.ShapeDtyp...]
where the time goes in v2:
time: 175 us; the launch traced here: 174 us
  Pallas kernels  166 us (95%)
  local copies, waits for them, and re-layouts  4.57 us (3%)
  other arithmetic  2.74 us (2%)
    pallas_call x1, Pallas kernels, weight_gradient(): pl.pallas_call(functools.partial(kernel, zs, xs), out_shape=jax.ShapeDtyp...  166 us
    unnamed x17, local copies, waits for them, and re-layouts  4.57 us

profile of v2, /device:TPU:1, one launch (start us, length us, event | category | flops | bytes accessed | tf_op | source)
XLA Modules:
  0.0 174.4 jit_solution(6139328550026505509)
XLA Ops:
  0.6 0.0 copy-start.3
  0.6 0.0 copy-start.4
  0.7 0.0 copy-start.5
  0.7 0.0 copy-start
  0.7 1.3 copy.18
  2.0 0.8 copy.21
  2.8 0.0 copy-done.3
  2.8 0.8 copy.17
  3.6 0.0 copy-done.4
  3.6 0.8 copy.19.noise_ref
  4.4 0.0 copy-done.5
  4.4 0.8 copy.20.target_ref
  5.2 0.0 copy-done
  5.2 0.7 bitcast_convert_fusion.ww_ref
  5.9 0.0 copy-start.1
  5.9 0.0 copy-start.2
  6.6 165.7 %weight_gradient.1 = f32[192,320]{1,0:T(8,128)} custom-call(s32[1]{0:T(128)S(6)} %copy.22.ts_ref, bf16[256,320]{1,0:T(8,128)(2,1)} %bitcast.35, bf16[256,3072]{1,0:T(8,128)(2,1)} %bitcast.33, bf16[192,320]{1,0:T(8,128)(2,1)} %bitcast_convert_fusion.ww_ref, bf16[160,1152]{1,0:T(8,128)(2,1)} %bitcast.34, bf16[192,320]{1,0:T(8,128)(2,1)} %to_ref.1, ...), custom_call_target="tpu_custom_call" | custom-call | tf_op jit(solution)/shard_map/weight_gradient/pallas_call | solution.py:880
  172.4 0.0 copy-done.1
  172.4 0.0 copy-done.2
  172.4 2.1 %fusion.3 = (f32[1,192,320]{2,1,0:T(8,128)}, f32[1,192,320]{2,1,0:T(8,128)}, f32[1,192,320]{2,1,0:T(8,128)}) fusion(f32[192,320]{1,0:T(8,128)} %weight_gradient.1, f32[1,192,320]{2,1,0:T(8,128)S(1)} %copy-done.1, f32[1,192,320]{2,1,0:T(8,128)S(1)} %copy-done.2, f32[1,192,320]{2,1,0:T(8,128)S(1)} %copy-done), kind=kLoop, calls=%fused_computation.7 | loop fusion | flops 737280 | bytes 1720320 | tf_op jit(solution)/shard_map/broadcast_in_dim | solution.py:918
Async XLA Ops:
  0.6 2.1 %copy-start.3 = (bf16[1,256,320]{1,2,0:T(8,128)(2,1)S(1)}, bf16[1,256,320]{1,2,0:T(8,128)(2,1)}, u32[]{:S(2)}) copy-start(bf16[1,256,320]{1,2,0:T(8,128)(2,1)} %param.10) | copy-start | bytes 491524
  0.6 3.0 %copy-start.4 = (bf16[256,320]{0,1:T(8,128)(2,1)S(1)}, bf16[256,320]{0,1:T(8,128)(2,1)}, u32[]{:S(2)}) copy-start(bf16[256,320]{0,1:T(8,128)(2,1)} %param.17) | copy-start | bytes 491524
  0.7 3.8 %copy-start.5 = (bf16[256,320]{0,1:T(8,128)(2,1)S(1)}, bf16[256,320]{0,1:T(8,128)(2,1)}, u32[]{:S(2)}) copy-start(bf16[256,320]{0,1:T(8,128)(2,1)} %param.19) | copy-start | bytes 491524
  0.7 4.6 %copy-start = (f32[1,192,320]{2,1,0:T(8,128)S(1)}, f32[1,192,320]{2,1,0:T(8,128)}, u32[]{:S(2)}) copy-start(f32[1,192,320]{2,1,0:T(8,128)} %param.12) | copy-start | bytes 737284
  5.9 166.4 %copy-start.1 = (f32[1,192,320]{2,1,0:T(8,128)S(1)}, f32[1,192,320]{2,1,0:T(8,128)}, u32[]{:S(2)}) copy-start(f32[1,192,320]{2,1,0:T(8,128)} %param.14) | copy-start | bytes 737284
  5.9 166.4 %copy-start.2 = (f32[1,192,320]{2,1,0:T(8,128)S(1)}, f32[1,192,320]{2,1,0:T(8,128)}, u32[]{:S(2)}) copy-start(f32[1,192,320]{2,1,0:T(8,128)} %param.13) | copy-start | bytes 737284

commit v3 on v2

--- a/solution.py
+++ b/solution.py
@@ -44,13 +44,17 @@
 
         self.start(ends, send_sem, recv_sem, device, when)
 
-    def finish(self):
-        for make, when in self.open:
+    def take(self):
+        taken, self.open = self.open, []
+        return taken
+
+    @staticmethod
+    def finish(taken):
+        for make, when in taken:
             if when is None:
                 make().wait_send()
             else:
                 pl.when(when)(lambda make=make: make().wait_send())
-        self.open = []
 
 
 def wait_recv(dst, recv_sem):
@@ -58,18 +62,20 @@
 
 
 class Ring:
-    def __init__(self, sends, place, buf, rows, sems, when=None, split=False):
+    def __init__(self, sends, place, buf, rows, sems, when=None, kind=None):
         self.sends, self.place, self.buf, self.rows, self.when = sends, place, buf, rows, when
-        self.split = split
+        self.kind = kind
         self.ring_send, self.ring_recv, self.pair_send, self.pair_recv = sems
         self.steps = place.zs // 2
 
     def piece(self, zz, cc, half):
-        if self.split:
+        if self.kind == 0:
             start = (2 * zz + cc) * self.rows
             return self.buf.at[half, pl.ds(pl.multiple_of(start, 16), self.rows)]
         each = self.rows // 2
         start = (2 * zz + cc) * self.rows + half * each
+        if self.kind == 1:
+            return self.buf.at[:, pl.ds(pl.multiple_of(start, 16), each), :]
         return self.buf.at[pl.ds(pl.multiple_of(start, 16), each)]
 
     def parts(self, k):
@@ -108,8 +114,10 @@
         for half in halves:
             self.pair(0, 0, half)
 
-    def advance(self, k):
+    def advance(self, k, halves=(0, 1)):
         for way, half in self.parts(k):
+            if half not in halves:
+                continue
             wait_recv(
                 self.piece(self.zz(k, way), self.place.c, half),
                 self.ring_recv.at[k - 1, way, half],
@@ -278,9 +286,9 @@
     p = Place(zs, xs)
     sends = Sends()
     tokens, inner = ho_ref.shape
-    cols = bi_ref.shape[1]
+    cols = bi_ref.shape[0]
     rows = ww_ref.shape[0]
-    depth = qw_ref.shape[0]
+    depth = qw_ref.shape[1]
     local_inner = q_hat.shape[1]
     heads = local_inner // HEAD_DIM
     steps = zs // 2
@@ -307,7 +315,7 @@
     swaps = [
         (ww_ref, lambda i: rows_of(w_buf.at[0], rows, i)),
         (bi_ref, lambda i: bi_t),
-        (qw_ref, lambda i: rows_of(q_buf, depth, i)),
+        (qw_ref, lambda i: q_buf.at[:, pl.ds(pl.multiple_of(i * depth, 16), depth), :]),
         (noise_ref, lambda i: noise_t),
         (to_ref, lambda i: rows_of(w_buf.at[1], rows, i)),
         (target_ref, lambda i: target_t),
@@ -404,14 +412,14 @@
                 when,
             )
 
-    def ring(buf, each, n, when=None, split=False):
+    def ring(buf, each, n, when=None, kind=None):
         sems = (ring_send.at[n], ring_recv.at[n], pair_send.at[n], pair_recv.at[n])
-        return Ring(sends, p, buf, each, sems, when, split)
+        return Ring(sends, p, buf, each, sems, when, kind)
 
     ring_w = ring(w_buf.at[0], rows, 0, first)
-    ring_qs = [ring(q_buf, depth, 1, first), ring(q_buf, depth, 1, second)]
-    ring_kv = ring(kv, tokens, 2, split=True)
-    ring_t = ring(w_buf.at[1], rows, 3)
+    ring_qs = [ring(q_buf, depth, 1, first, 1), ring(q_buf, depth, 1, second, 1)]
+    ring_kv = ring(kv, tokens, 2, kind=0)
+    ring_ts = [ring(w_buf.at[1], rows, 3, first), ring(w_buf.at[1], rows, 3, second)]
     over_noisy = Across(sends, p, noisy, (fan_send.at[0], fan_recv.at[0]))
     over_att = Across(sends, p, att, (fan_send.at[1], fan_recv.at[1]))
 
@@ -443,10 +451,11 @@
             wait_recv(gap_f.at[block], gf_recv.at[rank])
 
     def predict(which):
-        pred[...] = bi_t[...].astype(f32)
+        pred[...] = jnp.zeros_like(pred)
         project(lambda j, at: hob[p.c, :, at], which, pred)
 
     half_rows = [slice(0, tokens // 2), slice(tokens // 2, tokens)]
+    half_cols = [slice(0, cols // 2), slice(cols // 2, cols)]
 
     @pl.when(first)
     def _():
@@ -473,10 +482,10 @@
             ring_w.pair_arrived(k)
         swapped(1)
         predict(0)
-        gen[...] = pred[...].astype(jnp.bfloat16)
+        gen[...] = (bi_t[...].astype(f32) + pred[...].T).astype(jnp.bfloat16)
         for h in (0, 1):
             sends.start(
-                lambda h=h: (gen.at[half_rows[h]], gen_in.at[half_rows[h]]),
+                lambda h=h: (gen.at[half_cols[h]], gen_in.at[half_cols[h]]),
                 lambda h=h: one_send.at[h],
                 lambda h=h: one_recv.at[h],
                 lambda: p.dev(g=1),
@@ -501,11 +510,13 @@
         ring_q.advance(4)
         ho_forward(second_moved)
         own_ho.wait()
+        swapped(6)
+        ring_ts[1].begin()
 
     swapped(3)
     level = ts_ref[0].astype(f32) / 1000.0
     for h in (0, 1):
-        at = half_rows[h]
+        at = half_cols[h]
 
         @pl.when(second)
         def _():
@@ -519,6 +530,14 @@
 
     def first_q(k):
         pl.when(first)(lambda: ring_qs[0].advance(k))
+        pl.when(second)(lambda: ring_ts[1].advance(k))
+
+    def first_t(k):
+        pl.when(first)(lambda: ring_ts[0].advance(k))
+
+    @pl.when(first)
+    def _():
+        pred[...] = (gen[...].astype(f32) - noisy[p.block].astype(f32)).T
 
     over_noisy.forward(0, 0)
     first_q(1)
@@ -538,18 +557,13 @@
     def _():
         ho_arrived(second_moved)
 
-    def squares(f, total):
+    total = jnp.zeros((1, tokens), f32)
+    for f in range(fans):
         block = noisy[f].astype(f32)
-        return total + jnp.sum(block * block, axis=1, keepdims=True)
-
-    total = lax.fori_loop(0, fans, squares, jnp.zeros((tokens, 1), f32))
+        total += jnp.sum(block * block, axis=0, keepdims=True)
     factor = lax.rsqrt(total * (1.0 / (fans * cols)) + norm_eps)
-
-    def normalise(f, carry):
-        norm[f] = (noisy[f].astype(f32) * factor).astype(jnp.bfloat16)
-        return carry
-
-    lax.fori_loop(0, fans, normalise, 0)
+    for f in range(fans):
+        norm[f * cols : (f + 1) * cols, :] = (noisy[f].astype(f32) * factor).astype(jnp.bfloat16)
     first_q(4)
     for k in range(steps + 1):
         ring_qs[0].pair_arrived(k)
@@ -561,14 +575,9 @@
     own_rows = pl.ds(pl.multiple_of(home * tokens, 16), tokens)
 
     def proj(n):
-        value = jnp.zeros((tokens, local_inner), f32)
-        for f in range(fans):
-            value += jnp.dot(
-                norm[f],
-                q_buf[f * cols : (f + 1) * cols, n * local_inner : (n + 1) * local_inner],
-                preferred_element_type=f32,
-            )
-        return value
+        return lax.dot_general(
+            norm[...], q_buf[n], (((0,), (0,)), ((), ())), preferred_element_type=f32
+        )
 
     key_raw = proj(1)
     for h in range(heads):
@@ -607,15 +616,19 @@
     ring_kv.pair_arrived(0)
     attend(p.z)
     for k in range(1, steps + 1):
-        ring_kv.advance(k)
+        for half in (0, 1):
+            ring_kv.advance(k, (half,))
+            if k > 1:
+                if half == 0:
+                    ring_kv.pair_arrived(k - 1)
+                attend(ring_kv.zz(k - 1, half))
         if k == steps:
-            pl.when(first)(lambda: swapped(4))
-            pl.when(second)(lambda: swapped(6))
-            ring_t.begin()
-        if k > 1:
-            ring_kv.pair_arrived(k - 1)
-            for way in (0, 1):
-                attend(ring_kv.zz(k - 1, way))
+
+            @pl.when(first)
+            def _():
+                swapped(4)
+                ring_ts[0].begin()
+
     ring_kv.pair_arrived(steps)
     attend(ring_kv.zz(steps, 0))
 
@@ -628,19 +641,21 @@
             ).astype(jnp.bfloat16)
         over_att.begin(half)
     over_att.forward(0, 0)
-    ring_t.advance(1)
+    first_t(1)
     over_att.crossed(0)
     over_att.step(1, 0)
     over_att.forward(0, 1)
-    ring_t.advance(2)
+    first_t(2)
     over_att.crossed(1)
     over_att.step(1, 1)
     over_att.forward(1, 0)
-    ring_t.advance(3)
+    first_t(3)
     over_att.forward(1, 1)
-    ring_t.advance(4)
+    first_t(4)
     for k in range(steps + 1):
-        ring_t.pair_arrived(k)
+        ring_ts[0].pair_arrived(k)
+
+    early = sends.take()
 
     def pass_branch(h):
         sends.start(
@@ -677,16 +692,16 @@
         swapped(5)
         predict(1)
         grad[p.c] = (
-            (pred[...] - target_t[...].astype(f32)) * (1.0 / math.sqrt(tokens * 2 * zs))
+            (pred[...] + (bi_t[...].astype(f32) - target_t[...].astype(f32)).T) * (1.0 / math.sqrt(tokens * 2 * zs))
         ).astype(jnp.bfloat16)
 
     @pl.when(first)
     def _():
-        guess = noisy[p.block].astype(f32) + b_own[...]
-        gap = jnp.sum(jnp.abs(gen[...].astype(f32) - guess))
+        gap = jnp.sum(jnp.abs(pred[...] - b_own[...]))
         gap_f[p.block] = jnp.full((8, 128), gap, f32)
         gap_spread()
 
+    sends.finish(early)
     for h in (0, 1):
         rr = half_rows[h]
 
@@ -815,30 +830,29 @@
     def _():
         out_ref[...] = wg_out[...].astype(f32)
 
-    sends.finish()
+    sends.finish(sends.take())
 
 
 def weight_gradient(zs, xs, ts, bi, ho, ww, qw, to, noise, target, interpret=None):
     tokens, inner = ho.shape
-    cols = bi.shape[1]
+    cols = bi.shape[0]
     rows = ww.shape[0]
-    depth, triple = qw.shape
-    local_inner = triple // 3
+    depth, local_inner = qw.shape[1:]
     heads = local_inner // HEAD_DIM
     seq, fans, steps = 2 * zs, 2 * xs, zs // 2
     b16, f32 = jnp.bfloat16, jnp.float32
     vmem, dma = pltpu.VMEM, pltpu.SemaphoreType.DMA
     scratch = [
         vmem((2, inner, cols), b16),
-        vmem((seq * depth, triple), b16),
+        vmem((3, seq * depth, local_inner), b16),
         vmem((2, tokens, inner), b16),
-        vmem((tokens, cols), b16),
-        vmem((tokens, cols), b16),
-        vmem((tokens, cols), b16),
-        vmem((tokens, cols), b16),
-        vmem((tokens, cols), b16),
-        vmem((fans, tokens, cols), b16),
-        vmem((fans, tokens, cols), b16),
+        vmem((cols, tokens), b16),
+        vmem((cols, tokens), b16),
+        vmem((cols, tokens), b16),
+        vmem((cols, tokens), b16),
+        vmem((cols, tokens), b16),
+        vmem((fans, cols, tokens), b16),
+        vmem((fans * cols, tokens), b16),
         vmem((2, seq * tokens, local_inner), b16),
         vmem((tokens, local_inner), b16),
         vmem((tokens, local_inner), f32),
@@ -904,11 +918,10 @@
 ):
     zs, xs = lax.axis_size("seq") // 2, lax.axis_size("fsdp") // 2
     work_weight = out_master[0].astype(jnp.bfloat16)
-    triple = score_qkv.shape[1] * score_qkv.shape[2]
-    qw = score_qkv[0].reshape(triple, score_qkv.shape[3]).T
+    qw = score_qkv[0].transpose(0, 2, 1)
     weight_grad = weight_gradient(
-        zs, xs, timestep, block_input[0], head_outputs[0], work_weight, qw, teacher_out, noise,
-        fake_target,
+        zs, xs, timestep, block_input[0].T, head_outputs[0], work_weight, qw, teacher_out, noise.T,
+        fake_target.T,
     )
     new_first = 0.9 * first_moment[0] + 0.1 * weight_grad
     new_second = 0.95 * second_moment[0] + 0.05 * weight_grad * weight_grad

time: 175 us -> 163 us (0.931)
  Pallas kernels: 166 us -> 158 us
  local copies, waits for them, and re-layouts: 4.57 us -> 0.01 us
    pallas_call x1, Pallas kernels: 166 us -> 158 us  [weight_gradient(): pl.pallas_call(functools.partial(kernel, zs, xs), out_shape=jax.ShapeDtyp...]
    unnamed x17 -> x6, local copies, waits for them, and re-layouts: 4.57 us -> 0.01 us
where the time goes in v3:
time: 163 us
  Pallas kernels  158 us (97%)
  other arithmetic  3.7 us (2%)
    pallas_call x1, Pallas kernels, weight_gradient(): pl.pallas_call(functools.partial(kernel, zs, xs), out_shape=jax.ShapeDtyp...  158 us

profile of v3, /device:TPU:1, one launch (start us, length us, event | category | flops | bytes accessed | tf_op | source)
XLA Modules:
  0.0 162.7 jit_solution(8906298423045079648)
XLA Ops:
  1.3 1.6 %bitcast_convert_fusion.ww_ref = bf16[192,320]{1,0:T(8,128)(2,1)} fusion(f32[1,192,320]{2,1,0:T(8,128)} %param.12), kind=kLoop, calls=%fused_computation.4 | loop fusion | flops 61440 | bytes 368640 | tf_op jit(solution)/shard_map/convert_element_type | solution.py:920
  2.9 0.0 copy-start
  2.9 0.0 copy-start.1
  2.9 0.0 copy-start.2
  2.9 157.7 %weight_gradient.1 = f32[192,320]{1,0:T(8,128)} custom-call(s32[1]{0:T(128)S(6)} %copy.13.ts_ref, bf16[320,256]{1,0:T(8,128)(2,1)} %bitcast.34, bf16[256,3072]{1,0:T(8,128)(2,1)} %bitcast.32, bf16[192,320]{1,0:T(8,128)(2,1)} %bitcast_convert_fusion.ww_ref, bf16[3,160,384]{2,1,0:T(8,128)(2,1)} %bitcast.33, bf16[192,320]{1,0:T(8,128)(2,1)} %to_ref.1, ...), custom_call_target="tpu_custom_call" | custom-call | tf_op jit(solution)/shard_map/weight_gradient/pallas_call | solution.py:894
  160.6 0.0 copy-done
  160.6 0.0 copy-done.1
  160.6 0.0 copy-done.2
  160.6 2.1 %fusion.3 = (f32[1,192,320]{2,1,0:T(8,128)}, f32[1,192,320]{2,1,0:T(8,128)}, f32[1,192,320]{2,1,0:T(8,128)}) fusion(f32[192,320]{1,0:T(8,128)} %weight_gradient.1, f32[1,192,320]{2,1,0:T(8,128)S(1)} %copy-done.1, f32[1,192,320]{2,1,0:T(8,128)S(1)} %copy-done.2, f32[1,192,320]{2,1,0:T(8,128)S(1)} %copy-done), kind=kLoop, calls=%fused_computation.7 | loop fusion | flops 737280 | bytes 1720320 | tf_op jit(solution)/shard_map/broadcast_in_dim | solution.py:931
Async XLA Ops:
  2.9 157.7 %copy-start = (f32[1,192,320]{2,1,0:T(8,128)S(1)}, f32[1,192,320]{2,1,0:T(8,128)}, u32[]{:S(2)}) copy-start(f32[1,192,320]{2,1,0:T(8,128)} %param.12) | copy-start | bytes 737284
  2.9 157.7 %copy-start.1 = (f32[1,192,320]{2,1,0:T(8,128)S(1)}, f32[1,192,320]{2,1,0:T(8,128)}, u32[]{:S(2)}) copy-start(f32[1,192,320]{2,1,0:T(8,128)} %param.14) | copy-start | bytes 737284
  2.9 157.7 %copy-start.2 = (f32[1,192,320]{2,1,0:T(8,128)S(1)}, f32[1,192,320]{2,1,0:T(8,128)}, u32[]{:S(2)}) copy-start(f32[1,192,320]{2,1,0:T(8,128)} %param.13) | copy-start | bytes 737284

commit v4 on v3

--- a/solution.py
+++ b/solution.py
@@ -252,6 +252,9 @@
     lsum,
     att,
     pred,
+    gap_d,
+    grad_s,
+    hob_in,
     b_own,
     b_in,
     grad,
@@ -301,6 +304,7 @@
     peers = [p.dev(z=lax.rem(p.z + dz, zs)) for dz in range(1, zs)]
     peers += [p.beside(dx, da) for _, dx, da in p.fan()]
     peers += [p.dev(c=1 - p.c), p.dev(g=1 - p.g), p.dev(a=1 - p.a, c=1 - p.c)]
+    peers += [p.dev(g=1 - p.g, a=1 - p.a, c=1 - p.c)]
     for peer in peers:
         pl.semaphore_signal(barrier, inc=1, device_id=peer, device_id_type=MESH)
 
@@ -399,18 +403,11 @@
                     when,
                 )
 
-    def ho_arrived(when):
+    def ho_arrived():
         @pl.when(p.moved)
         def _():
             for way in (0, 1):
                 wait_recv(ho_rows(p.c, 2, way), ho_recv.at[3 + way])
-            sends.same(
-                lambda: hob.at[p.c],
-                lambda: ho_send.at[5],
-                lambda: ho_recv.at[5],
-                lambda: p.dev(c=1 - p.c),
-                when,
-            )
 
     def ring(buf, each, n, when=None, kind=None):
         sems = (ring_send.at[n], ring_recv.at[n], pair_send.at[n], pair_recv.at[n])
@@ -442,7 +439,7 @@
                 lambda rank=rank: gf_send.at[rank],
                 lambda rank=rank: gf_recv.at[rank],
                 lambda dx=dx, da=da: p.beside(dx, da),
-                first,
+                second,
             )
 
     def gap_gathered():
@@ -477,7 +474,7 @@
         swap(4, first_moved)
         ring_w.advance(4)
         own_ho.wait()
-        ho_arrived(first_moved)
+        ho_arrived()
         for k in range(steps + 1):
             ring_w.pair_arrived(k)
         swapped(1)
@@ -535,9 +532,9 @@
     def first_t(k):
         pl.when(first)(lambda: ring_ts[0].advance(k))
 
-    @pl.when(first)
+    @pl.when(second)
     def _():
-        pred[...] = (gen[...].astype(f32) - noisy[p.block].astype(f32)).T
+        gap_d[...] = (gen[...].astype(f32) - noisy[p.block].astype(f32)).T
 
     over_noisy.forward(0, 0)
     first_q(1)
@@ -555,7 +552,7 @@
 
     @pl.when(second)
     def _():
-        ho_arrived(second_moved)
+        ho_arrived()
 
     total = jnp.zeros((1, tokens), f32)
     for f in range(fans):
@@ -613,8 +610,35 @@
 
         lax.fori_loop(0, heads, one_head, 0)
 
+    early = sends.take()
+    sends.start(
+        lambda: (hob.at[p.c], hob_in.at[p.c]),
+        lambda: one_send.at[8],
+        lambda: one_recv.at[8],
+        lambda: p.dev(g=1 - p.g),
+    )
     ring_kv.pair_arrived(0)
     attend(p.z)
+
+    @pl.when(second)
+    def _():
+        for k in range(steps + 1):
+            ring_ts[1].pair_arrived(k)
+        swapped(1)
+        swapped(5)
+        predict(1)
+        grad_s[...] = (
+            (pred[...] + (bi_t[...].astype(f32) - target_t[...].astype(f32)).T)
+            * (1.0 / math.sqrt(tokens * 2 * zs))
+        ).astype(jnp.bfloat16)
+        sends.start(
+            lambda: (grad_s, grad.at[p.c]),
+            lambda: one_send.at[9],
+            lambda: one_recv.at[9],
+            lambda: p.dev(g=0),
+            second,
+        )
+
     for k in range(1, steps + 1):
         for half in (0, 1):
             ring_kv.advance(k, (half,))
@@ -622,6 +646,8 @@
                 if half == 0:
                     ring_kv.pair_arrived(k - 1)
                 attend(ring_kv.zz(k - 1, half))
+        if k == 2:
+            sends.finish(early)
         if k == steps:
 
             @pl.when(first)
@@ -652,9 +678,19 @@
     first_t(3)
     over_att.forward(1, 1)
     first_t(4)
-    for k in range(steps + 1):
-        ring_ts[0].pair_arrived(k)
-
+
+    @pl.when(first)
+    def _():
+        for k in range(steps + 1):
+            ring_ts[0].pair_arrived(k)
+
+    wait_recv(hob_in.at[p.c], one_recv.at[8])
+    sends.same(
+        lambda: hob_in.at[p.c],
+        lambda: one_send.at[10],
+        lambda: one_recv.at[10],
+        lambda: p.dev(c=1 - p.c),
+    )
     early = sends.take()
 
     def pass_branch(h):
@@ -662,8 +698,8 @@
             lambda: (b_own.at[half_rows[h]], b_in.at[half_rows[h]]),
             lambda: one_send.at[2 + h],
             lambda: one_recv.at[2 + h],
-            lambda: p.dev(g=0),
-            second,
+            lambda: p.dev(g=1),
+            first,
         )
 
     for h in (0, 1):
@@ -676,7 +712,7 @@
             )
         b_own[rr, :] = value
 
-        pl.when(second)(lambda: pass_branch(h))
+        pl.when(first)(lambda: pass_branch(h))
 
     def pass_grad(h):
         sends.same(
@@ -686,36 +722,27 @@
             lambda: p.dev(c=1 - p.c),
         )
 
+    @pl.when(first)
+    def _():
+        wait_recv(grad.at[p.c], one_recv.at[9])
+
+    for h in (0, 1):
+        rr = half_rows[h]
+
+        @pl.when(second)
+        def _():
+            wait_recv(b_in.at[rr], one_recv.at[2 + h])
+            grad[p.c, rr, :] = (b_own[rr, :] - b_in[rr, :]).astype(jnp.bfloat16)
+
+        pass_grad(h)
+
     @pl.when(second)
     def _():
-        swapped(1)
-        swapped(5)
-        predict(1)
-        grad[p.c] = (
-            (pred[...] + (bi_t[...].astype(f32) - target_t[...].astype(f32)).T) * (1.0 / math.sqrt(tokens * 2 * zs))
-        ).astype(jnp.bfloat16)
-
-    @pl.when(first)
-    def _():
-        gap = jnp.sum(jnp.abs(pred[...] - b_own[...]))
+        gap = jnp.sum(jnp.abs(gap_d[...] - b_in[...]))
         gap_f[p.block] = jnp.full((8, 128), gap, f32)
         gap_spread()
 
-    sends.finish(early)
-    for h in (0, 1):
-        rr = half_rows[h]
-
-        @pl.when(first)
-        def _():
-            wait_recv(b_in.at[rr], one_recv.at[2 + h])
-            grad[p.c, rr, :] = (b_in[rr, :] - b_own[rr, :]).astype(jnp.bfloat16)
-
-        pass_grad(h)
-
-    @pl.when(p.kept)
-    def _():
-        wait_recv(hob.at[1 - p.c], ho_recv.at[5])
-
+    wait_recv(hob_in.at[1 - p.c], one_recv.at[10])
     for h in (0, 1):
         wait_recv(grad.at[1 - p.c, half_rows[h]], one_recv.at[4 + h])
 
@@ -724,7 +751,7 @@
         value = jnp.zeros((wide, cols), f32)
         for block in range(2):
             value += lax.dot_general(
-                hob[block, :, at],
+                hob_in[block, :, at],
                 grad[block],
                 (((0,), (0,)), ((), ())),
                 preferred_element_type=f32,
@@ -732,22 +759,22 @@
         tmp[...] = value
         return tmp[pl.ds(pl.multiple_of(p.c * rows, 16), rows), :]
 
-    def span(j, way):
-        if j > 1:
-            return slice(0, rows)
-        return slice(0, rows // 2) if way == 0 else slice(rows // 2, rows)
-
-    def rs_start(j, way):
-        at = span(j, way)
+    each = rows // 2
+    half_chunk = [slice(0, each), slice(each, rows)]
+
+    def rs_parts(j):
+        return [(0, 0), (1, 1)] if j == 1 else [(0, 1), (1, 0), (0, 0), (1, 1)]
+
+    def rs_start(j, way, half):
         sends.start(
-            lambda: (rs_send.at[j - 1, way, at], rs_recv.at[j - 1, way, at]),
-            lambda: rs_ssem.at[j - 1, way],
-            lambda: rs_rsem.at[j - 1, way],
+            lambda: (rs_send.at[j - 1, way, half], rs_recv.at[j - 1, way, half]),
+            lambda: rs_ssem.at[j - 1, way, half],
+            lambda: rs_rsem.at[j - 1, way, half],
             lambda: p.dev(z=p.zp if way == 0 else p.zm),
         )
 
-    def rs_wait(j, way):
-        wait_recv(rs_recv.at[j - 1, way, span(j, way)], rs_rsem.at[j - 1, way])
+    def rs_wait(j, way, half):
+        wait_recv(rs_recv.at[j - 1, way, half], rs_rsem.at[j - 1, way, half])
 
     def gap_step(j):
         if j == 1:
@@ -759,7 +786,7 @@
                     lambda dz=dz: gz_send.at[dz],
                     lambda dz=dz: gz_recv.at[dz],
                     lambda dz=dz: p.dev(z=lax.rem(p.z + dz, zs)),
-                    first,
+                    second,
                 )
         if j == 2:
             for dz in range(1, zs):
@@ -770,66 +797,56 @@
                 lambda: one_send.at[6],
                 lambda: one_recv.at[6],
                 lambda: p.dev(c=1 - p.c),
-                first,
+                second,
             )
         if j == 3:
             wait_recv(gap_c.at[1 - p.c], one_recv.at[6])
 
     far = partial(lax.rem(p.z + steps, zs))
-    for way in (0, 1):
-        rs_send[0, way, span(1, way), :] = far[span(1, way)].astype(jnp.bfloat16)
-        rs_start(1, way)
-    pl.when(first)(lambda: gap_step(1))
+    for way, half in rs_parts(1):
+        rs_send[0, way, half] = far[half_chunk[half]].astype(jnp.bfloat16)
+        rs_start(1, way, half)
     for j in range(2, steps + 1):
-        for way in (0, 1):
-            dist = steps - j + 1
-            there = lax.rem(p.z + dist, zs) if way == 0 else lax.rem(p.z + zs - dist, zs)
-            mine = partial(there)
-            rs_wait(j - 1, way)
-            at = span(j - 1, way)
-            rs_send[j - 1, way] = mine.astype(jnp.bfloat16)
-            rs_send[j - 1, way, at, :] = (
-                mine[at] + rs_recv[j - 2, way, at, :].astype(f32)
-            ).astype(jnp.bfloat16)
-            rs_start(j, way)
+        dist = steps - j + 1
+        mine = [partial(lax.rem(p.z + dist, zs)), partial(lax.rem(p.z + zs - dist, zs))]
+        for way, half in rs_parts(j):
+            value = mine[way][half_chunk[half]]
+            if (way, half) in rs_parts(j - 1):
+                rs_wait(j - 1, way, half)
+                value = value + rs_recv[j - 2, way, half].astype(f32)
+            rs_send[j - 1, way, half] = value.astype(jnp.bfloat16)
+            rs_start(j, way, half)
         if j == 2:
-            pl.when(first)(lambda: gap_step(2))
-    if steps == 1:
-        pl.when(first)(lambda: gap_step(2))
+            pl.when(second)(lambda: gap_step(1))
+        if j == 3:
+            sends.finish(early)
+            pl.when(second)(lambda: gap_step(2))
     mine = partial(p.z)
-    pl.when(first)(lambda: gap_step(3))
+    pl.when(second)(lambda: gap_step(3))
     acc_w = tmp.at[0:rows]
     acc_w[...] = mine
-    for way in (0, 1):
-        rs_wait(steps, way)
-        at = span(steps, way)
-        acc_w[at, :] = acc_w[at, :] + rs_recv[steps - 1, way, at, :].astype(f32)
-
-    @pl.when(first)
+    for way, half in rs_parts(2):
+        rs_wait(steps, way, half)
+        at = half_chunk[half]
+        acc_w[at, :] = acc_w[at, :] + rs_recv[steps - 1, way, half].astype(f32)
+
+    @pl.when(second)
     def _():
         gap = (gap_c[0] + gap_c[1])[0:1, 0:1] * (1.0 / (tokens * 2 * zs * fans * cols))
         wg_out[...] = (acc_w[...] * (1.0 / (gap + norm_eps))).astype(jnp.bfloat16)
 
-    @pl.when(second)
+    @pl.when(first)
     def _():
         wg_out[...] = acc_w[...].astype(jnp.bfloat16)
 
-    @pl.when(p.moved)
-    def _():
-        sends.start(
-            lambda: (wg_out, wg_in),
-            lambda: one_send.at[7],
-            lambda: one_recv.at[7],
-            lambda: p.dev(a=p.c, c=p.a),
-            p.moved,
-        )
-        wait_recv(wg_in, one_recv.at[7])
-        out_ref[...] = wg_in[...].astype(f32)
-
-    @pl.when(p.kept)
-    def _():
-        out_ref[...] = wg_out[...].astype(f32)
-
+    sends.start(
+        lambda: (wg_out, wg_in),
+        lambda: one_send.at[7],
+        lambda: one_recv.at[7],
+        lambda: p.dev(g=1 - p.g, a=p.c, c=p.a),
+    )
+    wait_recv(wg_in, one_recv.at[7])
+    out_ref[...] = wg_in[...].astype(f32)
     sends.finish(sends.take())
 
 
@@ -860,11 +877,14 @@
         vmem((fans, tokens, local_inner), b16),
         vmem((tokens, cols), f32),
         vmem((tokens, cols), f32),
+        vmem((tokens, cols), b16),
+        vmem((2, tokens, inner), b16),
+        vmem((tokens, cols), f32),
         vmem((tokens, cols), f32),
         vmem((2, tokens, cols), b16),
         vmem((2 * rows, cols), f32),
-        vmem((steps, 2, rows, cols), b16),
-        vmem((steps, 2, rows, cols), b16),
+        vmem((steps, 2, 2, rows // 2, cols), b16),
+        vmem((steps, 2, 2, rows // 2, cols), b16),
         vmem((fans, 8, 128), f32),
         vmem((zs, 8, 128), f32),
         vmem((2, 8, 128), f32),
@@ -880,14 +900,14 @@
         dma((4, steps + 1, 2, 2)),
         dma((2, 18)),
         dma((2, 18)),
-        dma((steps, 2)),
-        dma((steps, 2)),
+        dma((steps, 2, 2)),
+        dma((steps, 2, 2)),
         dma((fans,)),
         dma((fans,)),
         dma((zs,)),
         dma((zs,)),
-        dma((8,)),
-        dma((8,)),
+        dma((11,)),
+        dma((11,)),
         dma((1,)),
     ]
     in_vmem = pl.BlockSpec(memory_space=pltpu.VMEM)

time: 163 us -> 167 us (1.025)
  Pallas kernels: 158 us -> 162 us
    pallas_call x1, Pallas kernels: 158 us -> 162 us  [weight_gradient(): pl.pallas_call(functools.partial(kernel, zs, xs), out_shape=jax.ShapeDtyp...]
where the time goes in v4:
time: 167 us
  Pallas kernels  162 us (97%)
  other arithmetic  3.7 us (2%)
    pallas_call x1, Pallas kernels, weight_gradient(): pl.pallas_call(functools.partial(kernel, zs, xs), out_shape=jax.ShapeDtyp...  162 us

profile of v4, /device:TPU:1, one launch (start us, length us, event | category | flops | bytes accessed | tf_op | source)
XLA Modules:
  0.0 166.7 jit_solution(15696245847612046364)
XLA Ops:
  1.3 1.6 bitcast_convert_fusion.ww_ref
  2.9 0.0 copy-start
  2.9 0.0 copy-start.1
  2.9 0.0 copy-start.2
  2.9 161.7 %weight_gradient.1 = f32[192,320]{1,0:T(8,128)} custom-call(s32[1]{0:T(128)S(6)} %copy.13.ts_ref, bf16[320,256]{1,0:T(8,128)(2,1)} %bitcast.34, bf16[256,3072]{1,0:T(8,128)(2,1)} %bitcast.32, bf16[192,320]{1,0:T(8,128)(2,1)} %bitcast_convert_fusion.ww_ref, bf16[3,160,384]{2,1,0:T(8,128)(2,1)} %bitcast.33, bf16[192,320]{1,0:T(8,128)(2,1)} %to_ref.1, ...), custom_call_target="tpu_custom_call" | custom-call | tf_op jit(solution)/shard_map/weight_gradient/pallas_call | solution.py:914
  164.6 0.0 copy-done
  164.6 0.0 copy-done.1
  164.6 0.0 copy-done.2
  164.6 2.1 %fusion.3 = (f32[1,192,320]{2,1,0:T(8,128)}, f32[1,192,320]{2,1,0:T(8,128)}, f32[1,192,320]{2,1,0:T(8,128)}) fusion(f32[192,320]{1,0:T(8,128)} %weight_gradient.1, f32[1,192,320]{2,1,0:T(8,128)S(1)} %copy-done.1, f32[1,192,320]{2,1,0:T(8,128)S(1)} %copy-done.2, f32[1,192,320]{2,1,0:T(8,128)S(1)} %copy-done), kind=kLoop, calls=%fused_computation.7 | loop fusion | flops 737280 | bytes 1720320 | tf_op jit(solution)/shard_map/broadcast_in_dim | solution.py:951
Async XLA Ops:
  2.9 161.7 %copy-start = (f32[1,192,320]{2,1,0:T(8,128)S(1)}, f32[1,192,320]{2,1,0:T(8,128)}, u32[]{:S(2)}) copy-start(f32[1,192,320]{2,1,0:T(8,128)} %param.12) | copy-start | bytes 737284
  2.9 161.7 %copy-start.1 = (f32[1,192,320]{2,1,0:T(8,128)S(1)}, f32[1,192,320]{2,1,0:T(8,128)}, u32[]{:S(2)}) copy-start(f32[1,192,320]{2,1,0:T(8,128)} %param.14) | copy-start | bytes 737284
  2.9 161.7 %copy-start.2 = (f32[1,192,320]{2,1,0:T(8,128)S(1)}, f32[1,192,320]{2,1,0:T(8,128)}, u32[]{:S(2)}) copy-start(f32[1,192,320]{2,1,0:T(8,128)} %param.13) | copy-start | bytes 737284

commit v5 on v3

--- a/solution.py
+++ b/solution.py
@@ -732,22 +732,22 @@
         tmp[...] = value
         return tmp[pl.ds(pl.multiple_of(p.c * rows, 16), rows), :]
 
-    def span(j, way):
-        if j > 1:
-            return slice(0, rows)
-        return slice(0, rows // 2) if way == 0 else slice(rows // 2, rows)
-
-    def rs_start(j, way):
-        at = span(j, way)
+    each = rows // 2
+    half_chunk = [slice(0, each), slice(each, rows)]
+
+    def rs_parts(j):
+        return [(0, 0), (1, 1)] if j == 1 else [(0, 1), (1, 0), (0, 0), (1, 1)]
+
+    def rs_start(j, way, half):
         sends.start(
-            lambda: (rs_send.at[j - 1, way, at], rs_recv.at[j - 1, way, at]),
-            lambda: rs_ssem.at[j - 1, way],
-            lambda: rs_rsem.at[j - 1, way],
+            lambda: (rs_send.at[j - 1, way, half], rs_recv.at[j - 1, way, half]),
+            lambda: rs_ssem.at[j - 1, way, half],
+            lambda: rs_rsem.at[j - 1, way, half],
             lambda: p.dev(z=p.zp if way == 0 else p.zm),
         )
 
-    def rs_wait(j, way):
-        wait_recv(rs_recv.at[j - 1, way, span(j, way)], rs_rsem.at[j - 1, way])
+    def rs_wait(j, way, half):
+        wait_recv(rs_recv.at[j - 1, way, half], rs_rsem.at[j - 1, way, half])
 
     def gap_step(j):
         if j == 1:
@@ -776,34 +776,31 @@
             wait_recv(gap_c.at[1 - p.c], one_recv.at[6])
 
     far = partial(lax.rem(p.z + steps, zs))
-    for way in (0, 1):
-        rs_send[0, way, span(1, way), :] = far[span(1, way)].astype(jnp.bfloat16)
-        rs_start(1, way)
-    pl.when(first)(lambda: gap_step(1))
+    for way, half in rs_parts(1):
+        rs_send[0, way, half] = far[half_chunk[half]].astype(jnp.bfloat16)
+        rs_start(1, way, half)
     for j in range(2, steps + 1):
-        for way in (0, 1):
-            dist = steps - j + 1
-            there = lax.rem(p.z + dist, zs) if way == 0 else lax.rem(p.z + zs - dist, zs)
-            mine = partial(there)
-            rs_wait(j - 1, way)
-            at = span(j - 1, way)
-            rs_send[j - 1, way] = mine.astype(jnp.bfloat16)
-            rs_send[j - 1, way, at, :] = (
-                mine[at] + rs_recv[j - 2, way, at, :].astype(f32)
-            ).astype(jnp.bfloat16)
-            rs_start(j, way)
+        dist = steps - j + 1
+        mine = [partial(lax.rem(p.z + dist, zs)), partial(lax.rem(p.z + zs - dist, zs))]
+        for way, half in rs_parts(j):
+            value = mine[way][half_chunk[half]]
+            if (way, half) in rs_parts(j - 1):
+                rs_wait(j - 1, way, half)
+                value = value + rs_recv[j - 2, way, half].astype(f32)
+            rs_send[j - 1, way, half] = value.astype(jnp.bfloat16)
+            rs_start(j, way, half)
         if j == 2:
+            pl.when(first)(lambda: gap_step(1))
+        if j == 3:
             pl.when(first)(lambda: gap_step(2))
-    if steps == 1:
-        pl.when(first)(lambda: gap_step(2))
     mine = partial(p.z)
     pl.when(first)(lambda: gap_step(3))
     acc_w = tmp.at[0:rows]
     acc_w[...] = mine
-    for way in (0, 1):
-        rs_wait(steps, way)
-        at = span(steps, way)
-        acc_w[at, :] = acc_w[at, :] + rs_recv[steps - 1, way, at, :].astype(f32)
+    for way, half in rs_parts(2):
+        rs_wait(steps, way, half)
+        at = half_chunk[half]
+        acc_w[at, :] = acc_w[at, :] + rs_recv[steps - 1, way, half].astype(f32)
 
     @pl.when(first)
     def _():
@@ -863,8 +860,8 @@
         vmem((tokens, cols), f32),
         vmem((2, tokens, cols), b16),
         vmem((2 * rows, cols), f32),
-        vmem((steps, 2, rows, cols), b16),
-        vmem((steps, 2, rows, cols), b16),
+        vmem((steps, 2, 2, rows // 2, cols), b16),
+        vmem((steps, 2, 2, rows // 2, cols), b16),
         vmem((fans, 8, 128), f32),
         vmem((zs, 8, 128), f32),
         vmem((2, 8, 128), f32),
@@ -880,8 +877,8 @@
         dma((4, steps + 1, 2, 2)),
         dma((2, 18)),
         dma((2, 18)),
-        dma((steps, 2)),
-        dma((steps, 2)),
+        dma((steps, 2, 2)),
+        dma((steps, 2, 2)),
         dma((fans,)),
         dma((fans,)),
         dma((zs,)),

time: 163 us -> 160 us (0.982)
  Pallas kernels: 158 us -> 154 us
    pallas_call x1, Pallas kernels: 158 us -> 154 us  [weight_gradient(): pl.pallas_call(functools.partial(kernel, zs, xs), out_shape=jax.ShapeDtyp...]
where the time goes in v5:
time: 160 us; the launch traced here: 159 us
  Pallas kernels  154 us (96%)
  other arithmetic  3.7 us (2%)
    pallas_call x1, Pallas kernels, weight_gradient(): pl.pallas_call(functools.partial(kernel, zs, xs), out_shape=jax.ShapeDtyp...  154 us

profile of v5, /device:TPU:1, one launch (start us, length us, event | category | flops | bytes accessed | tf_op | source)
XLA Modules:
  0.0 159.5 jit_solution(8362362882810382986)
XLA Ops:
  1.3 1.6 %bitcast_convert_fusion.ww_ref = bf16[192,320]{1,0:T(8,128)(2,1)} fusion(f32[1,192,320]{2,1,0:T(8,128)} %param.12), kind=kLoop, calls=%fused_computation.4 | loop fusion | flops 61440 | bytes 368640 | tf_op jit(solution)/shard_map/convert_element_type | solution.py:917
  2.9 0.0 copy-start
  2.9 0.0 copy-start.1
  2.9 0.0 copy-start.2
  2.9 154.5 %weight_gradient.1 = f32[192,320]{1,0:T(8,128)} custom-call(s32[1]{0:T(128)S(6)} %copy.13.ts_ref, bf16[320,256]{1,0:T(8,128)(2,1)} %bitcast.34, bf16[256,3072]{1,0:T(8,128)(2,1)} %bitcast.32, bf16[192,320]{1,0:T(8,128)(2,1)} %bitcast_convert_fusion.ww_ref, bf16[3,160,384]{2,1,0:T(8,128)(2,1)} %bitcast.33, bf16[192,320]{1,0:T(8,128)(2,1)} %to_ref.1, ...), custom_call_target="tpu_custom_call" | custom-call | tf_op jit(solution)/shard_map/weight_gradient/pallas_call | solution.py:891
  157.4 0.0 copy-done
  157.4 0.0 copy-done.1
  157.4 0.0 copy-done.2
  157.4 2.1 %fusion.3 = (f32[1,192,320]{2,1,0:T(8,128)}, f32[1,192,320]{2,1,0:T(8,128)}, f32[1,192,320]{2,1,0:T(8,128)}) fusion(f32[192,320]{1,0:T(8,128)} %weight_gradient.1, f32[1,192,320]{2,1,0:T(8,128)S(1)} %copy-done.1, f32[1,192,320]{2,1,0:T(8,128)S(1)} %copy-done.2, f32[1,192,320]{2,1,0:T(8,128)S(1)} %copy-done), kind=kLoop, calls=%fused_computation.7 | loop fusion | flops 737280 | bytes 1720320 | tf_op jit(solution)/shard_map/broadcast_in_dim | solution.py:928
Async XLA Ops:
  2.9 154.5 %copy-start = (f32[1,192,320]{2,1,0:T(8,128)S(1)}, f32[1,192,320]{2,1,0:T(8,128)}, u32[]{:S(2)}) copy-start(f32[1,192,320]{2,1,0:T(8,128)} %param.12) | copy-start | bytes 737284
  2.9 154.5 %copy-start.1 = (f32[1,192,320]{2,1,0:T(8,128)S(1)}, f32[1,192,320]{2,1,0:T(8,128)}, u32[]{:S(2)}) copy-start(f32[1,192,320]{2,1,0:T(8,128)} %param.14) | copy-start | bytes 737284
  2.9 154.5 %copy-start.2 = (f32[1,192,320]{2,1,0:T(8,128)S(1)}, f32[1,192,320]{2,1,0:T(8,128)}, u32[]{:S(2)}) copy-start(f32[1,192,320]{2,1,0:T(8,128)} %param.13) | copy-start | bytes 737284

commit v6 on v5

--- a/solution.py
+++ b/solution.py
@@ -502,16 +502,7 @@
         ring_q.advance(1)
         swap(6, second_moved)
         ring_q.advance(2)
-        ho_cross(second_kept)
-        swap(1, second_moved)
-        ring_q.advance(3)
-        ho_step(second_moved)
-        swap(5, second_moved)
-        ring_q.advance(4)
-        ho_forward(second_moved)
         own_ho.wait()
-        swapped(6)
-        ring_ts[1].begin()
 
     swapped(3)
     level = ts_ref[0].astype(f32) / 1000.0
@@ -530,7 +521,31 @@
 
     def first_q(k):
         pl.when(first)(lambda: ring_qs[0].advance(k))
-        pl.when(second)(lambda: ring_ts[1].advance(k))
+
+        @pl.when(second)
+        def _():
+            if k == 1:
+                ring_qs[1].advance(3)
+            if k == 2:
+                ring_qs[1].advance(4)
+                swapped(6)
+                ring_ts[1].begin()
+            if k == 4:
+                ring_ts[1].advance(1)
+
+    def second_later(k):
+        if k == 0:
+            ho_cross(second_kept)
+            swap(1, second_moved)
+            swap(5, second_moved)
+        if k == 1:
+            ho_step(second_moved)
+        if k == 2:
+            ho_forward(second_moved)
+        if k == 3:
+            ho_arrived(second_moved)
+        if 1 <= k <= 3:
+            ring_ts[1].advance(k + 1)
 
     def first_t(k):
         pl.when(first)(lambda: ring_ts[0].advance(k))
@@ -553,10 +568,6 @@
     over_noisy.arrived(0)
     over_noisy.arrived(1)
 
-    @pl.when(second)
-    def _():
-        ho_arrived(second_moved)
-
     total = jnp.zeros((1, tokens), f32)
     for f in range(fans):
         block = noisy[f].astype(f32)
@@ -615,6 +626,7 @@
 
     ring_kv.pair_arrived(0)
     attend(p.z)
+    pl.when(second)(lambda: second_later(0))
     for k in range(1, steps + 1):
         for half in (0, 1):
             ring_kv.advance(k, (half,))
@@ -622,6 +634,7 @@
                 if half == 0:
                     ring_kv.pair_arrived(k - 1)
                 attend(ring_kv.zz(k - 1, half))
+        pl.when(second)(lambda: second_later(k))
         if k == steps:
 
             @pl.when(first)

time: 160 us -> 158 us (0.988)
  no operation moved by 1% of the time
where the time goes in v6:
time: 158 us
  Pallas kernels  153 us (97%)
  other arithmetic  3.7 us (2%)
    pallas_call x1, Pallas kernels, weight_gradient(): pl.pallas_call(functools.partial(kernel, zs, xs), out_shape=jax.ShapeDtyp...  153 us

profile of v6, /device:TPU:1, one launch (start us, length us, event | category | flops | bytes accessed | tf_op | source)
XLA Modules:
  0.0 158.1 jit_solution(18302139670120767765)
XLA Ops:
  1.3 1.6 %bitcast_convert_fusion.ww_ref = bf16[192,320]{1,0:T(8,128)(2,1)} fusion(f32[1,192,320]{2,1,0:T(8,128)} %param.12), kind=kLoop, calls=%fused_computation.4 | loop fusion | flops 61440 | bytes 368640 | tf_op jit(solution)/shard_map/convert_element_type | solution.py:930
  2.9 0.0 copy-start
  2.9 0.0 copy-start.1
  2.9 0.0 copy-start.2
  2.9 153.0 %weight_gradient.1 = f32[192,320]{1,0:T(8,128)} custom-call(s32[1]{0:T(128)S(6)} %copy.13.ts_ref, bf16[320,256]{1,0:T(8,128)(2,1)} %bitcast.34, bf16[256,3072]{1,0:T(8,128)(2,1)} %bitcast.32, bf16[192,320]{1,0:T(8,128)(2,1)} %bitcast_convert_fusion.ww_ref, bf16[3,160,384]{2,1,0:T(8,128)(2,1)} %bitcast.33, bf16[192,320]{1,0:T(8,128)(2,1)} %to_ref.1, ...), custom_call_target="tpu_custom_call" | custom-call | tf_op jit(solution)/shard_map/weight_gradient/pallas_call | solution.py:904
  156.0 0.0 copy-done
  156.0 0.0 copy-done.1
  156.0 0.0 copy-done.2
  156.0 2.1 %fusion.3 = (f32[1,192,320]{2,1,0:T(8,128)}, f32[1,192,320]{2,1,0:T(8,128)}, f32[1,192,320]{2,1,0:T(8,128)}) fusion(f32[192,320]{1,0:T(8,128)} %weight_gradient.1, f32[1,192,320]{2,1,0:T(8,128)S(1)} %copy-done.1, f32[1,192,320]{2,1,0:T(8,128)S(1)} %copy-done.2, f32[1,192,320]{2,1,0:T(8,128)S(1)} %copy-done), kind=kLoop, calls=%fused_computation.7 | loop fusion | flops 737280 | bytes 1720320 | tf_op jit(solution)/shard_map/broadcast_in_dim | solution.py:941
Async XLA Ops:
  2.9 153.0 %copy-start = (f32[1,192,320]{2,1,0:T(8,128)S(1)}, f32[1,192,320]{2,1,0:T(8,128)}, u32[]{:S(2)}) copy-start(f32[1,192,320]{2,1,0:T(8,128)} %param.12) | copy-start | bytes 737284
  2.9 153.1 %copy-start.1 = (f32[1,192,320]{2,1,0:T(8,128)S(1)}, f32[1,192,320]{2,1,0:T(8,128)}, u32[]{:S(2)}) copy-start(f32[1,192,320]{2,1,0:T(8,128)} %param.14) | copy-start | bytes 737284
  2.9 153.1 %copy-start.2 = (f32[1,192,320]{2,1,0:T(8,128)S(1)}, f32[1,192,320]{2,1,0:T(8,128)}, u32[]{:S(2)}) copy-start(f32[1,192,320]{2,1,0:T(8,128)} %param.13) | copy-start | bytes 737284

commit v7 on v6

--- a/solution.py
+++ b/solution.py
@@ -462,13 +462,13 @@
         ring_q = ring_qs[0]
         swap(0, first_moved)
         ho_cross(first_kept)
-        swap(1, first_moved)
         swapped(0)
         ring_w.begin()
-        swap(3, first_moved)
-        swap(2, first_moved)
         ring_w.advance(1)
         ho_step(first_moved)
+        swap(2, first_moved)
+        swap(1, first_moved)
+        swap(3, first_moved)
         ring_w.advance(2)
         ring_w.advance(3)
         ho_forward(first_moved)

time: 158 us -> 158 us (level)
  no operation moved by 1% of the time
where the time goes in v7:
time: 158 us
  Pallas kernels  153 us (97%)
  other arithmetic  3.7 us (2%)
    pallas_call x1, Pallas kernels, weight_gradient(): pl.pallas_call(functools.partial(kernel, zs, xs), out_shape=jax.ShapeDtyp...  153 us

profile of v7, /device:TPU:1, one launch (start us, length us, event | category | flops | bytes accessed | tf_op | source)
XLA Modules:
  0.0 158.1 jit_solution(6861272922185632357)
XLA Ops:
  1.3 1.6 %bitcast_convert_fusion.ww_ref = bf16[192,320]{1,0:T(8,128)(2,1)} fusion(f32[1,192,320]{2,1,0:T(8,128)} %param.12), kind=kLoop, calls=%fused_computation.4 | loop fusion | flops 61440 | bytes 368640 | tf_op jit(solution)/shard_map/convert_element_type | solution.py:930
  2.9 0.0 copy-start
  2.9 0.0 copy-start.1
  2.9 0.0 copy-start.2
  2.9 153.0 %weight_gradient.1 = f32[192,320]{1,0:T(8,128)} custom-call(s32[1]{0:T(128)S(6)} %copy.13.ts_ref, bf16[320,256]{1,0:T(8,128)(2,1)} %bitcast.34, bf16[256,3072]{1,0:T(8,128)(2,1)} %bitcast.32, bf16[192,320]{1,0:T(8,128)(2,1)} %bitcast_convert_fusion.ww_ref, bf16[3,160,384]{2,1,0:T(8,128)(2,1)} %bitcast.33, bf16[192,320]{1,0:T(8,128)(2,1)} %to_ref.1, ...), custom_call_target="tpu_custom_call" | custom-call | tf_op jit(solution)/shard_map/weight_gradient/pallas_call | solution.py:904
  156.0 0.0 copy-done
  156.0 0.0 copy-done.1
  156.0 0.0 copy-done.2
  156.0 2.1 %fusion.3 = (f32[1,192,320]{2,1,0:T(8,128)}, f32[1,192,320]{2,1,0:T(8,128)}, f32[1,192,320]{2,1,0:T(8,128)}) fusion(f32[192,320]{1,0:T(8,128)} %weight_gradient.1, f32[1,192,320]{2,1,0:T(8,128)S(1)} %copy-done.1, f32[1,192,320]{2,1,0:T(8,128)S(1)} %copy-done.2, f32[1,192,320]{2,1,0:T(8,128)S(1)} %copy-done), kind=kLoop, calls=%fused_computation.7 | loop fusion | flops 737280 | bytes 1720320 | tf_op jit(solution)/shard_map/broadcast_in_dim | solution.py:941
Async XLA Ops:
  2.9 153.0 %copy-start = (f32[1,192,320]{2,1,0:T(8,128)S(1)}, f32[1,192,320]{2,1,0:T(8,128)}, u32[]{:S(2)}) copy-start(f32[1,192,320]{2,1,0:T(8,128)} %param.12) | copy-start | bytes 737284
  2.9 153.1 %copy-start.1 = (f32[1,192,320]{2,1,0:T(8,128)S(1)}, f32[1,192,320]{2,1,0:T(8,128)}, u32[]{:S(2)}) copy-start(f32[1,192,320]{2,1,0:T(8,128)} %param.14) | copy-start | bytes 737284
  2.9 153.1 %copy-start.2 = (f32[1,192,320]{2,1,0:T(8,128)S(1)}, f32[1,192,320]{2,1,0:T(8,128)}, u32[]{:S(2)}) copy-start(f32[1,192,320]{2,1,0:T(8,128)} %param.13) | copy-start | bytes 737284

commit v8 on v6

--- a/solution.py
+++ b/solution.py
@@ -425,16 +425,6 @@
 
     wide = 2 * rows
 
-    def project(lhs, which, out):
-        def part(j, carry):
-            at = pl.ds(pl.multiple_of(j * wide, 128), wide)
-            out[...] += jnp.dot(
-                lhs(j, at), w_buf[which, at, :], preferred_element_type=f32
-            )
-            return carry
-
-        lax.fori_loop(0, inner // wide, part, 0)
-
     def gap_spread():
         for rank, dx, da in p.fan():
             sends.same(
@@ -451,8 +441,11 @@
             wait_recv(gap_f.at[block], gf_recv.at[rank])
 
     def predict(which):
-        pred[...] = jnp.zeros_like(pred)
-        project(lambda j, at: hob[p.c, :, at], which, pred)
+        value = jnp.zeros((tokens, cols), f32)
+        for j in range(inner // wide):
+            at = slice(j * wide, (j + 1) * wide)
+            value += jnp.dot(hob[p.c, :, at], w_buf[which, at, :], preferred_element_type=f32)
+        pred[...] = value
 
     half_rows = [slice(0, tokens // 2), slice(tokens // 2, tokens)]
     half_cols = [slice(0, cols // 2), slice(cols // 2, cols)]

time: 158 us -> 157 us (level)
  no operation moved by 1% of the time
where the time goes in v8:
time: 157 us
  Pallas kernels  152 us (97%)
  other arithmetic  3.7 us (2%)
    pallas_call x1, Pallas kernels, weight_gradient(): pl.pallas_call(functools.partial(kernel, zs, xs), out_shape=jax.ShapeDtyp...  152 us

profile of v8, /device:TPU:1, one launch (start us, length us, event | category | flops | bytes accessed | tf_op | source)
XLA Modules:
  0.0 156.9 jit_solution(149162877774580668)
XLA Ops:
  1.3 1.6 %bitcast_convert_fusion.ww_ref = bf16[192,320]{1,0:T(8,128)(2,1)} fusion(f32[1,192,320]{2,1,0:T(8,128)} %param.12), kind=kLoop, calls=%fused_computation.4 | loop fusion | flops 61440 | bytes 368640 | tf_op jit(solution)/shard_map/convert_element_type | solution.py:923
  2.9 0.0 copy-start
  2.9 0.0 copy-start.1
  2.9 0.0 copy-start.2
  2.9 151.9 %weight_gradient.1 = f32[192,320]{1,0:T(8,128)} custom-call(s32[1]{0:T(128)S(6)} %copy.13.ts_ref, bf16[320,256]{1,0:T(8,128)(2,1)} %bitcast.34, bf16[256,3072]{1,0:T(8,128)(2,1)} %bitcast.32, bf16[192,320]{1,0:T(8,128)(2,1)} %bitcast_convert_fusion.ww_ref, bf16[3,160,384]{2,1,0:T(8,128)(2,1)} %bitcast.33, bf16[192,320]{1,0:T(8,128)(2,1)} %to_ref.1, ...), custom_call_target="tpu_custom_call" | custom-call | tf_op jit(solution)/shard_map/weight_gradient/pallas_call | solution.py:897
  154.8 0.0 copy-done
  154.8 0.0 copy-done.1
  154.8 0.0 copy-done.2
  154.9 2.1 %fusion.3 = (f32[1,192,320]{2,1,0:T(8,128)}, f32[1,192,320]{2,1,0:T(8,128)}, f32[1,192,320]{2,1,0:T(8,128)}) fusion(f32[192,320]{1,0:T(8,128)} %weight_gradient.1, f32[1,192,320]{2,1,0:T(8,128)S(1)} %copy-done.1, f32[1,192,320]{2,1,0:T(8,128)S(1)} %copy-done.2, f32[1,192,320]{2,1,0:T(8,128)S(1)} %copy-done), kind=kLoop, calls=%fused_computation.7 | loop fusion | flops 737280 | bytes 1720320 | tf_op jit(solution)/shard_map/broadcast_in_dim | solution.py:934
Async XLA Ops:
  2.9 151.9 %copy-start = (f32[1,192,320]{2,1,0:T(8,128)S(1)}, f32[1,192,320]{2,1,0:T(8,128)}, u32[]{:S(2)}) copy-start(f32[1,192,320]{2,1,0:T(8,128)} %param.12) | copy-start | bytes 737284
  2.9 151.9 %copy-start.1 = (f32[1,192,320]{2,1,0:T(8,128)S(1)}, f32[1,192,320]{2,1,0:T(8,128)}, u32[]{:S(2)}) copy-start(f32[1,192,320]{2,1,0:T(8,128)} %param.14) | copy-start | bytes 737284
  2.9 151.9 %copy-start.2 = (f32[1,192,320]{2,1,0:T(8,128)S(1)}, f32[1,192,320]{2,1,0:T(8,128)}, u32[]{:S(2)}) copy-start(f32[1,192,320]{2,1,0:T(8,128)} %param.13) | copy-start | bytes 737284
